TPU v7x, 32 devices: a whole 2x2x4 slice. The times are simulated.
32 devices in a mesh: grp: 2 (over y), sub: 4 (over z), shot: 4 (over x, core).
Axes of the slice: x: 2, y: 2, z: 4, core: 2. Of those that a mesh axis runs over, the one named last changes fastest.
Arguments:
- model_field: float32 [32, 256, 128], P(('grp', 'sub')), parts along dimension 0, may hold values from 0.08 to 0.22
- source_index: int32 [8, 256], P(('grp', 'shot')), parts along dimension 0, may hold values from 0 to 524287
- wavelets: float32 [8, 12, 256], P(('grp', 'shot')), parts along dimension 0, may hold values from -6 to 6
- receiver_index: int32 [8, 512], P(('grp', 'shot')), parts along dimension 0, may hold values from 0 to 524287
- observed: float32 [8, 12, 512], P(('grp', 'shot')), parts along dimension 0, may hold values from -6 to 6
Outputs:
- updated_model: float32 [32, 256, 128], P(('grp', 'sub')), parts along dimension 0
- gradient: float32 [32, 256, 128], P(('grp', 'sub'), 'shot'), parts along dimension 0
There are 2 independent parts, one for each index of `grp`. A program takes and returns all parts, laid end to end along the dimension named above; each array names one. Nothing has to cross between parts.
All inputs are finite; a program needn't handle non-finite values.
Results may differ from a plain program's by a relative error of at most 0.00002.
Values sent between devices are 32-bit elements; how exact they have to be, the bound alone decides.
A program may use at most 64 MiB of HBM per device.

v0:
```python
import jax
import jax.numpy as jnp
from jax import lax
from jax.sharding import PartitionSpec as P

ITERS = 6


near_weight = 4.0 / 3.0
far_weight = -1.0 / 12.0
centre_weight = 7.5
step_length = 0.02
tv_bound = 0.01
dual_step = 0.25
primal_step = 0.25
lower_bound = 0.08
upper_bound = 0.22
epsilon = 1e-06


def padded_2(shard, sides, width):
    for axis, dim in sides:
        size, length = (lax.axis_size(axis), shard.shape[dim])
        up = [(i, (i + 1) % size) for i in range(size - 1)]
        down = [(j, i) for i, j in up]
        last = lax.slice_in_dim(shard, length - width, length, axis=dim)
        initial = lax.slice_in_dim(shard, 0, width, axis=dim)
        before = lax.ppermute(last, axis, up)
        after = lax.ppermute(initial, axis, down)
        shard = jnp.concatenate([before, shard, after], axis=dim)
    return shard


def from_behind(value, axis, steps):
    count = lax.axis_size(axis)
    initial, last = (max(0, -steps), min(count, count - steps))
    return lax.ppermute(value, axis, [(source, source + steps) for source in range(initial, last)])


def laplacian(padded):
    centre = padded[..., 2:-2, 2:-2, 2:-2]
    near = (
        padded[..., 3:-1, 2:-2, 2:-2]
        + padded[..., 1:-3, 2:-2, 2:-2]
        + padded[..., 2:-2, 3:-1, 2:-2]
        + padded[..., 2:-2, 1:-3, 2:-2]
        + padded[..., 2:-2, 2:-2, 3:-1]
        + padded[..., 2:-2, 2:-2, 1:-3]
    )
    far = (
        padded[..., 4:, 2:-2, 2:-2]
        + padded[..., :-4, 2:-2, 2:-2]
        + padded[..., 2:-2, 4:, 2:-2]
        + padded[..., 2:-2, :-4, 2:-2]
        + padded[..., 2:-2, 2:-2, 4:]
        + padded[..., 2:-2, 2:-2, :-4]
    )
    return near_weight * near + far_weight * far - centre_weight * centre


def forward_part(field, along, upper, last_owner):
    size = field.shape[along]
    first_row = lax.slice_in_dim(field, 0, 1, axis=along)
    remainder = lax.slice_in_dim(field, 1, size, axis=along)
    beyond = jnp.zeros_like(first_row) if upper is None else upper(first_row)
    difference = jnp.concatenate([remainder, beyond], along) - field
    row_index = lax.broadcasted_iota(jnp.int32, field.shape, along)
    return jnp.where(jnp.logical_and(row_index == size - 1, last_owner), 0.0, difference)


def backward_part(dual, along, lower):
    size = dual.shape[along]
    last_row = lax.slice_in_dim(dual, size - 1, size, axis=along)
    before = jnp.zeros_like(last_row) if lower is None else lower(last_row)
    earlier = jnp.concatenate([before, lax.slice_in_dim(dual, 0, size - 1, axis=along)], along)
    return earlier - dual


def project(target, upper_x, lower_x, last_x):
    field = jnp.clip(target, lower_bound, upper_bound)
    extrap = field
    duals = [jnp.zeros_like(field) for along in range(3)]
    for iteration in range(ITERS):
        duals = [
            jnp.clip(
                duals[0] + dual_step * forward_part(extrap, 0, upper_x, last_x), -tv_bound, tv_bound
            ),
            jnp.clip(
                duals[1] + dual_step * forward_part(extrap, 1, None, True), -tv_bound, tv_bound
            ),
            jnp.clip(
                duals[2] + dual_step * forward_part(extrap, 2, None, True), -tv_bound, tv_bound
            ),
        ]
        adjoint = (
            backward_part(duals[0], 0, lower_x)
            + backward_part(duals[1], 1, None)
            + backward_part(duals[2], 2, None)
        )
        following = jnp.clip(
            (field - primal_step * adjoint + primal_step * target) / (1.0 + primal_step),
            lower_bound,
            upper_bound,
        )
        extrap = 2.0 * following - field
        field = following
    return field


def per_device(model_field, source_index, wavelets, receiver_index, observed):
    shot_count = source_index.shape[0]
    rows_x, rows_y, rows_z = model_field.shape
    cell_count = rows_x * rows_y * rows_z
    offset = lax.axis_index("sub") * cell_count
    pad_widths = ((0, 0), (0, 0), (2, 2), (2, 2))

    def localize(flat_index):
        local_slot = flat_index - offset
        inside = jnp.logical_and(local_slot >= 0, local_slot < cell_count)
        return (jnp.where(inside, local_slot, 0), inside.astype(jnp.float32))

    source_slot, source_inside = localize(source_index)
    receiver_slot, receiver_inside = localize(receiver_index)

    def stencil(current):
        padded = padded_2(current, (("sub", 1),), 2)
        interior = laplacian(jnp.pad(current, pad_widths))
        lower_rim = laplacian(jnp.pad(padded[:, :6], pad_widths))
        upper_rim = laplacian(jnp.pad(padded[:, -6:], pad_widths))
        return jnp.concatenate([lower_rim, interior, upper_rim], 1)

    inject = jax.vmap(lambda flat_field, slots, amounts: flat_field.at[slots].add(amounts))
    sample_at = jax.vmap(lambda flat_field, slots: flat_field[slots])
    shape = (shot_count, rows_x, rows_y, rows_z)

    def advance(earlier, current, slots, amounts):
        stored = stencil(current)
        following = 2.0 * current - earlier + model_field * stored
        following = inject(following.reshape(shot_count, -1), slots, amounts).reshape(shape)
        return (stored, following)

    def forward(state, wave_now):
        earlier, current = state
        stored, following = advance(earlier, current, source_slot, wave_now * source_inside)
        record = sample_at(following.reshape(shot_count, -1), receiver_slot) * receiver_inside
        return ((current, following), (stored, record))

    blank = jnp.zeros(shape, jnp.float32)
    _, (laps, record) = lax.scan(forward, (blank, blank), jnp.swapaxes(wavelets, 0, 1))
    misfit = (record - jnp.swapaxes(observed, 0, 1)) * receiver_inside

    def backward(state, inputs):
        earlier, current, gradient_sum = state
        stored, misfit_now = inputs
        unused, following = advance(earlier, current, receiver_slot, misfit_now)
        return ((current, following, gradient_sum + following * stored), None)

    (_, _, gradient_sum), _ = lax.scan(backward, (blank, blank, blank), (laps[::-1], misfit[::-1]))
    local_gradient = jnp.sum(gradient_sum, 0)
    last_x = lax.axis_index("sub") == lax.axis_size("sub") - 1
    slab_gradient = lax.psum(local_gradient, "shot")
    square_sum = lax.psum(jnp.sum(slab_gradient * slab_gradient), "sub")
    grad_scale = jnp.sqrt(square_sum / (cell_count * lax.axis_size("sub")) + epsilon)
    target = model_field - step_length * (slab_gradient / grad_scale)

    def slab_upper(layer):
        return from_behind(layer, "sub", -1)

    def slab_lower(layer):
        return from_behind(layer, "sub", 1)

    updated_model = project(target, slab_upper, slab_lower, last_x)
    brick_rows = rows_y // lax.axis_size("shot")
    gradient = lax.dynamic_slice_in_dim(
        slab_gradient, lax.axis_index("shot") * brick_rows, brick_rows, 1
    )
    return (updated_model, gradient)


def solution(mesh):
    placed = (
        P(("grp", "sub"), None, None),
        P(("grp", "shot"), None),
        P(("grp", "shot"), None, None),
        P(("grp", "shot"), None),
        P(("grp", "shot"), None, None),
    )
    return jax.shard_map(
        per_device,
        mesh=mesh,
        in_specs=placed,
        out_specs=(P(("grp", "sub"), None, None), P(("grp", "sub"), "shot", None)),
        check_vma=False,
    )
```

profile of v0, /device:TPU:0, one launch (start us, length us, event | category | flops | bytes accessed | tf_op | source)
XLA Modules:
  0.0 583.3 jit_solution(8010761035833371209)
XLA Ops:
  10.1 222.8 %while.35 = (s32[]{:T(128)}, f32[1,4,256,128]{3,2,1,0:T(8,128)S(1)}, f32[1,4,256,128]{3,2,1,0:T(8,128)S(1)}, f32[12,1,4,256,128]{4,3,2,1,0:T(8,128)}, f32[12,1,5...) while((s32[]{:T(128)}, ...), condition=%wide.region_2.3_spmd, body=%wide.region_0.2_spmd.sunk | while | flops 2758914 | bytes 17609972 | solution.py:149
  10.1 5.1 collective-permute-start
  20.8 4.0 collective-permute-done.1
  28.9 3.5 gather_fusion
  32.5 3.6 collective-permute-start
  40.5 4.0 collective-permute-done.1
  48.6 3.5 gather_fusion
  52.2 3.5 collective-permute-start
  59.7 4.3 collective-permute-done.1
  68.0 3.5 gather_fusion
  77.8 4.3 collective-permute-done.1
  95.7 4.3 collective-permute-done.1
  113.6 4.3 collective-permute-done.1
  131.5 4.3 collective-permute-done.1
  139.9 3.5 gather_fusion
  149.4 4.3 collective-permute-done.1
  167.3 4.3 collective-permute-done.1
  185.2 4.3 collective-permute-done.1
  193.5 3.5 gather_fusion
  203.1 4.3 collective-permute-done.1
  221.1 4.3 collective-permute-done.1
  229.4 3.5 gather_fusion
  233.0 6.2 %rev.7 = f32[12,1,4,256,128]{4,3,2,1,0:T(8,128)} reverse(f32[12,1,4,256,128]{4,3,2,1,0:T(8,128)} %get-tuple-element.242), dimensions={0} | reverse | bytes 12582912 | tf_op jit(solution)/shard_map/rev | solution.py:158
  239.2 200.9 %while.36 = (s32[]{:T(128)}, f32[1,4,256,128]{3,2,1,0:T(8,128)S(1)}, f32[1,4,256,128]{3,2,1,0:T(8,128)S(1)}, f32[1,4,256,128]{3,2,1,0:T(8,128)S(1)}, f32[4,256,1...) while((s32[]{:T(128)}, ...), condition=%wide.region_5.6_spmd.clone, body=%wide.region_3.5_spmd.clone.sunk | while | flops 3017731 | bytes 16543951 | solution.py:158
  242.6 4.8 collective-permute-done.2
  247.4 4.5 collective-permute-done.3
  252.8 3.6 scatter_fusion.1
  261.1 4.6 collective-permute-done.2
  265.8 4.0 collective-permute-done.3
  270.7 3.6 scatter_fusion.1
  279.5 3.8 collective-permute-done.2
  283.4 4.0 collective-permute-done.3
  288.2 3.6 scatter_fusion.1
  299.9 4.0 collective-permute-done.3
  304.8 3.6 scatter_fusion.1
  316.2 4.3 collective-permute-done.3
  321.3 3.6 scatter_fusion.1
  332.6 4.3 collective-permute-done.3
  337.8 3.6 scatter_fusion.1
  348.8 4.3 collective-permute-done.3
  354.0 3.6 scatter_fusion.1
  365.0 4.3 collective-permute-done.3
  370.2 3.6 scatter_fusion.1
  381.3 4.3 collective-permute-done.3
  386.4 3.6 scatter_fusion.1
  397.5 4.3 collective-permute-done.3
  402.6 3.6 scatter_fusion.1
  413.7 4.3 collective-permute-done.3
  418.8 3.6 scatter_fusion.1
  429.9 4.3 collective-permute-done.3
  435.0 3.6 scatter_fusion.1
  440.9 32.7 %all-reduce.30.cloned.1.call-done = f32[4,256,128]{2,1,0:T(8,128)} async-done(((f32[4,256,128]{2,1,0:T(8,128)}), f32[4,256,128]{2,1,0:T(8,128)}) %all-reduce.30.cloned.1.call-update) | async-done | bytes 524304 | tf_op jit(solution)/shard_map/psum | solution.py:161
  475.5 12.3 %psum.15 = f32[]{:T(128)} all-reduce(f32[]{:T(128)} %multiply_reduce_fusion), channel_id=1, replica_groups=mesh['grp'=2,'sub'=4,'shot'=4] {'sub'}, use_global_device_ids=true, to_apply=%region_8.9 | all-reduce | flops 1 | bytes 8 | tf_op jit(solution)/shard_map/psum | solution.py:162
  491.3 5.3 collective-permute-done.4
  502.9 5.7 collective-permute-done.6
  509.0 3.9 collective-permute-start.7
  517.4 5.7 collective-permute-done.8
  523.4 3.9 collective-permute-start.9
  531.9 5.7 collective-permute-done.10
  537.9 3.9 collective-permute-start.11
  546.8 7.1 %collective-permute-done.12 = f32[1,256,128]{2,1,0:T(8,128)S(1)} collective-permute-done((f32[1,256,128]{2,1,0:T(8,128)S(1)}, f32[1,256,128]{2,1,0:T(8,128)S(1)}, u32[]{:S(2)}, u32[]{:S(2)}) %collective-permute-start.12) | collective-permute-done | bytes 131104 | tf_op jit(solution)/shard_map/ppermute | solution.py:37
  554.2 3.8 collective-permute-start.13
  562.8 5.7 collective-permute-done.14
  568.9 3.9 collective-permute-start.15
  (556 shorter events, 266.7 us)
Async XLA Ops:
  7.2 466.5 %all-reduce.30.cloned.1.call-start = ((), (), s32[]{:S(2)}) async-start(), calls=%async_computation | async-start | bytes 1048576 | tf_op jit(solution)/shard_map/psum | solution.py:161
  10.0 222.9 %copy-start.3 = (f32[1,12,512]{2,0,1:T(1,128)S(1)}, f32[1,12,512]{2,0,1:T(1,128)}, u32[]{:S(2)}) copy-start(f32[1,12,512]{2,0,1:T(1,128)} %param.13) | copy-start | bytes 73732
  10.1 16.3 %copy-start = (f32[4,256,128]{2,1,0:T(8,128)S(1)}, f32[4,256,128]{2,1,0:T(8,128)}, u32[]{:S(2)}) copy-start(f32[4,256,128]{2,1,0:T(8,128)} %get-tuple-element.520) | copy-start | bytes 1572868 | tf_op jit(solution)/shard_map/while
  10.1 10.6 %collective-permute-start = (f32[1,2,256,128]{3,2,1,0:T(8,128)S(1)}, f32[1,2,256,128]{3,2,1,0:T(8,128)S(1)}, u32[]{:S(2)}, u32[]{:S(2)}) collective-permute-start(f32[1,2,256,128]{3,2,1,0:T(8,128)S(1)} %get-tuple-element.471), channel_id=1, source_target_pairs={{0,4},{4,8},{8,12},{1,5},{5,9},{9,13},{2,6},{6,10},{10,14},{3,7},{... | collective-permute-start | bytes 786440 | tf_op jit(solution)/shard_map/while/body/eval_jaxpr/ppermute | solution.py:28
  15.2 9.7 %collective-permute-start.1 = (f32[1,2,256,128]{3,2,1,0:T(8,128)S(1)}, f32[1,2,256,128]{3,2,1,0:T(8,128)S(1)}, u32[]{:S(2)}, u32[]{:S(2)}) collective-permute-start(f32[1,2,256,128]{3,2,1,0:T(8,128)S(1)} %get-tuple-element.473), channel_id=1, source_target_pairs={{4,0},{8,4},{12,8},{5,1},{9,5},{13,9},{6,2},{10,6},{14,10},{7,3},{... | collective-permute-start | bytes 786440 | tf_op jit(solution)/shard_map/while/body/eval_jaxpr/ppermute | solution.py:29
  32.4 13.6 %copy-start = (f32[4,256,128]{2,1,0:T(8,128)S(1)}, f32[4,256,128]{2,1,0:T(8,128)}, u32[]{:S(2)}) copy-start(f32[4,256,128]{2,1,0:T(8,128)} %get-tuple-element.520) | copy-start | bytes 1572868 | tf_op jit(solution)/shard_map/while
  32.5 7.9 %collective-permute-start = (f32[1,2,256,128]{3,2,1,0:T(8,128)S(1)}, f32[1,2,256,128]{3,2,1,0:T(8,128)S(1)}, u32[]{:S(2)}, u32[]{:S(2)}) collective-permute-start(f32[1,2,256,128]{3,2,1,0:T(8,128)S(1)} %get-tuple-element.471), channel_id=1, source_target_pairs={{0,4},{4,8},{8,12},{1,5},{5,9},{9,13},{2,6},{6,10},{10,14},{3,7},{... | collective-permute-start | bytes 786440 | tf_op jit(solution)/shard_map/while/body/eval_jaxpr/ppermute | solution.py:28
  36.1 8.5 %collective-permute-start.1 = (f32[1,2,256,128]{3,2,1,0:T(8,128)S(1)}, f32[1,2,256,128]{3,2,1,0:T(8,128)S(1)}, u32[]{:S(2)}, u32[]{:S(2)}) collective-permute-start(f32[1,2,256,128]{3,2,1,0:T(8,128)S(1)} %get-tuple-element.473), channel_id=1, source_target_pairs={{4,0},{8,4},{12,8},{5,1},{9,5},{13,9},{6,2},{10,6},{14,10},{7,3},{... | collective-permute-start | bytes 786440 | tf_op jit(solution)/shard_map/while/body/eval_jaxpr/ppermute | solution.py:29
  52.2 7.4 %collective-permute-start = (f32[1,2,256,128]{3,2,1,0:T(8,128)S(1)}, f32[1,2,256,128]{3,2,1,0:T(8,128)S(1)}, u32[]{:S(2)}, u32[]{:S(2)}) collective-permute-start(f32[1,2,256,128]{3,2,1,0:T(8,128)S(1)} %get-tuple-element.471), channel_id=1, source_target_pairs={{0,4},{4,8},{8,12},{1,5},{5,9},{9,13},{2,6},{6,10},{10,14},{3,7},{... | collective-permute-start | bytes 786440 | tf_op jit(solution)/shard_map/while/body/eval_jaxpr/ppermute | solution.py:28
  55.7 8.3 %collective-permute-start.1 = (f32[1,2,256,128]{3,2,1,0:T(8,128)S(1)}, f32[1,2,256,128]{3,2,1,0:T(8,128)S(1)}, u32[]{:S(2)}, u32[]{:S(2)}) collective-permute-start(f32[1,2,256,128]{3,2,1,0:T(8,128)S(1)} %get-tuple-element.473), channel_id=1, source_target_pairs={{4,0},{8,4},{12,8},{5,1},{9,5},{13,9},{6,2},{10,6},{14,10},{7,3},{... | collective-permute-start | bytes 786440 | tf_op jit(solution)/shard_map/while/body/eval_jaxpr/ppermute | solution.py:29
  71.6 6.2 %collective-permute-start = (f32[1,2,256,128]{3,2,1,0:T(8,128)S(1)}, f32[1,2,256,128]{3,2,1,0:T(8,128)S(1)}, u32[]{:S(2)}, u32[]{:S(2)}) collective-permute-start(f32[1,2,256,128]{3,2,1,0:T(8,128)S(1)} %get-tuple-element.471), channel_id=1, source_target_pairs={{0,4},{4,8},{8,12},{1,5},{5,9},{9,13},{2,6},{6,10},{10,14},{3,7},{... | collective-permute-start | bytes 786440 | tf_op jit(solution)/shard_map/while/body/eval_jaxpr/ppermute | solution.py:28
  73.9 8.3 %collective-permute-start.1 = (f32[1,2,256,128]{3,2,1,0:T(8,128)S(1)}, f32[1,2,256,128]{3,2,1,0:T(8,128)S(1)}, u32[]{:S(2)}, u32[]{:S(2)}) collective-permute-start(f32[1,2,256,128]{3,2,1,0:T(8,128)S(1)} %get-tuple-element.473), channel_id=1, source_target_pairs={{4,0},{8,4},{12,8},{5,1},{9,5},{13,9},{6,2},{10,6},{14,10},{7,3},{... | collective-permute-start | bytes 786440 | tf_op jit(solution)/shard_map/while/body/eval_jaxpr/ppermute | solution.py:29
  89.7 5.9 %collective-permute-start = (f32[1,2,256,128]{3,2,1,0:T(8,128)S(1)}, f32[1,2,256,128]{3,2,1,0:T(8,128)S(1)}, u32[]{:S(2)}, u32[]{:S(2)}) collective-permute-start(f32[1,2,256,128]{3,2,1,0:T(8,128)S(1)} %get-tuple-element.471), channel_id=1, source_target_pairs={{0,4},{4,8},{8,12},{1,5},{5,9},{9,13},{2,6},{6,10},{10,14},{3,7},{... | collective-permute-start | bytes 786440 | tf_op jit(solution)/shard_map/while/body/eval_jaxpr/ppermute | solution.py:28
  91.8 8.3 %collective-permute-start.1 = (f32[1,2,256,128]{3,2,1,0:T(8,128)S(1)}, f32[1,2,256,128]{3,2,1,0:T(8,128)S(1)}, u32[]{:S(2)}, u32[]{:S(2)}) collective-permute-start(f32[1,2,256,128]{3,2,1,0:T(8,128)S(1)} %get-tuple-element.473), channel_id=1, source_target_pairs={{4,0},{8,4},{12,8},{5,1},{9,5},{13,9},{6,2},{10,6},{14,10},{7,3},{... | collective-permute-start | bytes 786440 | tf_op jit(solution)/shard_map/while/body/eval_jaxpr/ppermute | solution.py:29
  107.6 5.9 %collective-permute-start = (f32[1,2,256,128]{3,2,1,0:T(8,128)S(1)}, f32[1,2,256,128]{3,2,1,0:T(8,128)S(1)}, u32[]{:S(2)}, u32[]{:S(2)}) collective-permute-start(f32[1,2,256,128]{3,2,1,0:T(8,128)S(1)} %get-tuple-element.471), channel_id=1, source_target_pairs={{0,4},{4,8},{8,12},{1,5},{5,9},{9,13},{2,6},{6,10},{10,14},{3,7},{... | collective-permute-start | bytes 786440 | tf_op jit(solution)/shard_map/while/body/eval_jaxpr/ppermute | solution.py:28
  109.7 8.3 %collective-permute-start.1 = (f32[1,2,256,128]{3,2,1,0:T(8,128)S(1)}, f32[1,2,256,128]{3,2,1,0:T(8,128)S(1)}, u32[]{:S(2)}, u32[]{:S(2)}) collective-permute-start(f32[1,2,256,128]{3,2,1,0:T(8,128)S(1)} %get-tuple-element.473), channel_id=1, source_target_pairs={{4,0},{8,4},{12,8},{5,1},{9,5},{13,9},{6,2},{10,6},{14,10},{7,3},{... | collective-permute-start | bytes 786440 | tf_op jit(solution)/shard_map/while/body/eval_jaxpr/ppermute | solution.py:29
  125.5 5.9 %collective-permute-start = (f32[1,2,256,128]{3,2,1,0:T(8,128)S(1)}, f32[1,2,256,128]{3,2,1,0:T(8,128)S(1)}, u32[]{:S(2)}, u32[]{:S(2)}) collective-permute-start(f32[1,2,256,128]{3,2,1,0:T(8,128)S(1)} %get-tuple-element.471), channel_id=1, source_target_pairs={{0,4},{4,8},{8,12},{1,5},{5,9},{9,13},{2,6},{6,10},{10,14},{3,7},{... | collective-permute-start | bytes 786440 | tf_op jit(solution)/shard_map/while/body/eval_jaxpr/ppermute | solution.py:28
  127.6 8.3 %collective-permute-start.1 = (f32[1,2,256,128]{3,2,1,0:T(8,128)S(1)}, f32[1,2,256,128]{3,2,1,0:T(8,128)S(1)}, u32[]{:S(2)}, u32[]{:S(2)}) collective-permute-start(f32[1,2,256,128]{3,2,1,0:T(8,128)S(1)} %get-tuple-element.473), channel_id=1, source_target_pairs={{4,0},{8,4},{12,8},{5,1},{9,5},{13,9},{6,2},{10,6},{14,10},{7,3},{... | collective-permute-start | bytes 786440 | tf_op jit(solution)/shard_map/while/body/eval_jaxpr/ppermute | solution.py:29
  143.4 5.9 %collective-permute-start = (f32[1,2,256,128]{3,2,1,0:T(8,128)S(1)}, f32[1,2,256,128]{3,2,1,0:T(8,128)S(1)}, u32[]{:S(2)}, u32[]{:S(2)}) collective-permute-start(f32[1,2,256,128]{3,2,1,0:T(8,128)S(1)} %get-tuple-element.471), channel_id=1, source_target_pairs={{0,4},{4,8},{8,12},{1,5},{5,9},{9,13},{2,6},{6,10},{10,14},{3,7},{... | collective-permute-start | bytes 786440 | tf_op jit(solution)/shard_map/while/body/eval_jaxpr/ppermute | solution.py:28
  145.5 8.3 %collective-permute-start.1 = (f32[1,2,256,128]{3,2,1,0:T(8,128)S(1)}, f32[1,2,256,128]{3,2,1,0:T(8,128)S(1)}, u32[]{:S(2)}, u32[]{:S(2)}) collective-permute-start(f32[1,2,256,128]{3,2,1,0:T(8,128)S(1)} %get-tuple-element.473), channel_id=1, source_target_pairs={{4,0},{8,4},{12,8},{5,1},{9,5},{13,9},{6,2},{10,6},{14,10},{7,3},{... | collective-permute-start | bytes 786440 | tf_op jit(solution)/shard_map/while/body/eval_jaxpr/ppermute | solution.py:29
  161.3 5.9 %collective-permute-start = (f32[1,2,256,128]{3,2,1,0:T(8,128)S(1)}, f32[1,2,256,128]{3,2,1,0:T(8,128)S(1)}, u32[]{:S(2)}, u32[]{:S(2)}) collective-permute-start(f32[1,2,256,128]{3,2,1,0:T(8,128)S(1)} %get-tuple-element.471), channel_id=1, source_target_pairs={{0,4},{4,8},{8,12},{1,5},{5,9},{9,13},{2,6},{6,10},{10,14},{3,7},{... | collective-permute-start | bytes 786440 | tf_op jit(solution)/shard_map/while/body/eval_jaxpr/ppermute | solution.py:28
  163.4 8.3 %collective-permute-start.1 = (f32[1,2,256,128]{3,2,1,0:T(8,128)S(1)}, f32[1,2,256,128]{3,2,1,0:T(8,128)S(1)}, u32[]{:S(2)}, u32[]{:S(2)}) collective-permute-start(f32[1,2,256,128]{3,2,1,0:T(8,128)S(1)} %get-tuple-element.473), channel_id=1, source_target_pairs={{4,0},{8,4},{12,8},{5,1},{9,5},{13,9},{6,2},{10,6},{14,10},{7,3},{... | collective-permute-start | bytes 786440 | tf_op jit(solution)/shard_map/while/body/eval_jaxpr/ppermute | solution.py:29
  179.2 5.9 %collective-permute-start = (f32[1,2,256,128]{3,2,1,0:T(8,128)S(1)}, f32[1,2,256,128]{3,2,1,0:T(8,128)S(1)}, u32[]{:S(2)}, u32[]{:S(2)}) collective-permute-start(f32[1,2,256,128]{3,2,1,0:T(8,128)S(1)} %get-tuple-element.471), channel_id=1, source_target_pairs={{0,4},{4,8},{8,12},{1,5},{5,9},{9,13},{2,6},{6,10},{10,14},{3,7},{... | collective-permute-start | bytes 786440 | tf_op jit(solution)/shard_map/while/body/eval_jaxpr/ppermute | solution.py:28
  181.3 8.3 %collective-permute-start.1 = (f32[1,2,256,128]{3,2,1,0:T(8,128)S(1)}, f32[1,2,256,128]{3,2,1,0:T(8,128)S(1)}, u32[]{:S(2)}, u32[]{:S(2)}) collective-permute-start(f32[1,2,256,128]{3,2,1,0:T(8,128)S(1)} %get-tuple-element.473), channel_id=1, source_target_pairs={{4,0},{8,4},{12,8},{5,1},{9,5},{13,9},{6,2},{10,6},{14,10},{7,3},{... | collective-permute-start | bytes 786440 | tf_op jit(solution)/shard_map/while/body/eval_jaxpr/ppermute | solution.py:29
  197.1 5.9 %collective-permute-start = (f32[1,2,256,128]{3,2,1,0:T(8,128)S(1)}, f32[1,2,256,128]{3,2,1,0:T(8,128)S(1)}, u32[]{:S(2)}, u32[]{:S(2)}) collective-permute-start(f32[1,2,256,128]{3,2,1,0:T(8,128)S(1)} %get-tuple-element.471), channel_id=1, source_target_pairs={{0,4},{4,8},{8,12},{1,5},{5,9},{9,13},{2,6},{6,10},{10,14},{3,7},{... | collective-permute-start | bytes 786440 | tf_op jit(solution)/shard_map/while/body/eval_jaxpr/ppermute | solution.py:28
  199.2 8.3 %collective-permute-start.1 = (f32[1,2,256,128]{3,2,1,0:T(8,128)S(1)}, f32[1,2,256,128]{3,2,1,0:T(8,128)S(1)}, u32[]{:S(2)}, u32[]{:S(2)}) collective-permute-start(f32[1,2,256,128]{3,2,1,0:T(8,128)S(1)} %get-tuple-element.473), channel_id=1, source_target_pairs={{4,0},{8,4},{12,8},{5,1},{9,5},{13,9},{6,2},{10,6},{14,10},{7,3},{... | collective-permute-start | bytes 786440 | tf_op jit(solution)/shard_map/while/body/eval_jaxpr/ppermute | solution.py:29
  215.1 5.9 %collective-permute-start = (f32[1,2,256,128]{3,2,1,0:T(8,128)S(1)}, f32[1,2,256,128]{3,2,1,0:T(8,128)S(1)}, u32[]{:S(2)}, u32[]{:S(2)}) collective-permute-start(f32[1,2,256,128]{3,2,1,0:T(8,128)S(1)} %get-tuple-element.471), channel_id=1, source_target_pairs={{0,4},{4,8},{8,12},{1,5},{5,9},{9,13},{2,6},{6,10},{10,14},{3,7},{... | collective-permute-start | bytes 786440 | tf_op jit(solution)/shard_map/while/body/eval_jaxpr/ppermute | solution.py:28
  217.1 8.3 %collective-permute-start.1 = (f32[1,2,256,128]{3,2,1,0:T(8,128)S(1)}, f32[1,2,256,128]{3,2,1,0:T(8,128)S(1)}, u32[]{:S(2)}, u32[]{:S(2)}) collective-permute-start(f32[1,2,256,128]{3,2,1,0:T(8,128)S(1)} %get-tuple-element.473), channel_id=1, source_target_pairs={{4,0},{8,4},{12,8},{5,1},{9,5},{13,9},{6,2},{10,6},{14,10},{7,3},{... | collective-permute-start | bytes 786440 | tf_op jit(solution)/shard_map/while/body/eval_jaxpr/ppermute | solution.py:29
  239.3 8.0 %collective-permute-start.2 = (f32[1,2,256,128]{3,2,1,0:T(8,128)S(1)}, f32[1,2,256,128]{3,2,1,0:T(8,128)S(1)}, u32[]{:S(2)}, u32[]{:S(2)}) collective-permute-start(f32[1,2,256,128]{3,2,1,0:T(8,128)S(1)} %get-tuple-element.485), channel_id=1, source_target_pairs={{0,4},{4,8},{8,12},{1,5},{5,9},{9,13},{2,6},{6,10},{10,14},{3,7},{... | collective-permute-start | bytes 786440 | tf_op jit(solution)/shard_map/while/body/eval_jaxpr/ppermute | solution.py:28
  241.2 10.8 %collective-permute-start.3 = (f32[1,2,256,128]{3,2,1,0:T(8,128)S(1)}, f32[1,2,256,128]{3,2,1,0:T(8,128)S(1)}, u32[]{:S(2)}, u32[]{:S(2)}) collective-permute-start(f32[1,2,256,128]{3,2,1,0:T(8,128)S(1)} %get-tuple-element.487), channel_id=1, source_target_pairs={{4,0},{8,4},{12,8},{5,1},{9,5},{13,9},{6,2},{10,6},{14,10},{7,3},{... | collective-permute-start | bytes 786440 | tf_op jit(solution)/shard_map/while/body/eval_jaxpr/ppermute | solution.py:29
  257.9 7.8 %collective-permute-start.2 = (f32[1,2,256,128]{3,2,1,0:T(8,128)S(1)}, f32[1,2,256,128]{3,2,1,0:T(8,128)S(1)}, u32[]{:S(2)}, u32[]{:S(2)}) collective-permute-start(f32[1,2,256,128]{3,2,1,0:T(8,128)S(1)} %get-tuple-element.485), channel_id=1, source_target_pairs={{0,4},{4,8},{8,12},{1,5},{5,9},{9,13},{2,6},{6,10},{10,14},{3,7},{... | collective-permute-start | bytes 786440 | tf_op jit(solution)/shard_map/while/body/eval_jaxpr/ppermute | solution.py:28
  259.7 10.1 %collective-permute-start.3 = (f32[1,2,256,128]{3,2,1,0:T(8,128)S(1)}, f32[1,2,256,128]{3,2,1,0:T(8,128)S(1)}, u32[]{:S(2)}, u32[]{:S(2)}) collective-permute-start(f32[1,2,256,128]{3,2,1,0:T(8,128)S(1)} %get-tuple-element.487), channel_id=1, source_target_pairs={{4,0},{8,4},{12,8},{5,1},{9,5},{13,9},{6,2},{10,6},{14,10},{7,3},{... | collective-permute-start | bytes 786440 | tf_op jit(solution)/shard_map/while/body/eval_jaxpr/ppermute | solution.py:29
  275.8 7.4 %collective-permute-start.2 = (f32[1,2,256,128]{3,2,1,0:T(8,128)S(1)}, f32[1,2,256,128]{3,2,1,0:T(8,128)S(1)}, u32[]{:S(2)}, u32[]{:S(2)}) collective-permute-start(f32[1,2,256,128]{3,2,1,0:T(8,128)S(1)} %get-tuple-element.485), channel_id=1, source_target_pairs={{0,4},{4,8},{8,12},{1,5},{5,9},{9,13},{2,6},{6,10},{10,14},{3,7},{... | collective-permute-start | bytes 786440 | tf_op jit(solution)/shard_map/while/body/eval_jaxpr/ppermute | solution.py:28
  278.1 9.3 %collective-permute-start.3 = (f32[1,2,256,128]{3,2,1,0:T(8,128)S(1)}, f32[1,2,256,128]{3,2,1,0:T(8,128)S(1)}, u32[]{:S(2)}, u32[]{:S(2)}) collective-permute-start(f32[1,2,256,128]{3,2,1,0:T(8,128)S(1)} %get-tuple-element.487), channel_id=1, source_target_pairs={{4,0},{8,4},{12,8},{5,1},{9,5},{13,9},{6,2},{10,6},{14,10},{7,3},{... | collective-permute-start | bytes 786440 | tf_op jit(solution)/shard_map/while/body/eval_jaxpr/ppermute | solution.py:29
  293.3 6.5 %collective-permute-start.2 = (f32[1,2,256,128]{3,2,1,0:T(8,128)S(1)}, f32[1,2,256,128]{3,2,1,0:T(8,128)S(1)}, u32[]{:S(2)}, u32[]{:S(2)}) collective-permute-start(f32[1,2,256,128]{3,2,1,0:T(8,128)S(1)} %get-tuple-element.485), channel_id=1, source_target_pairs={{0,4},{4,8},{8,12},{1,5},{5,9},{9,13},{2,6},{6,10},{10,14},{3,7},{... | collective-permute-start | bytes 786440 | tf_op jit(solution)/shard_map/while/body/eval_jaxpr/ppermute | solution.py:28
  295.6 8.3 %collective-permute-start.3 = (f32[1,2,256,128]{3,2,1,0:T(8,128)S(1)}, f32[1,2,256,128]{3,2,1,0:T(8,128)S(1)}, u32[]{:S(2)}, u32[]{:S(2)}) collective-permute-start(f32[1,2,256,128]{3,2,1,0:T(8,128)S(1)} %get-tuple-element.487), channel_id=1, source_target_pairs={{4,0},{8,4},{12,8},{5,1},{9,5},{13,9},{6,2},{10,6},{14,10},{7,3},{... | collective-permute-start | bytes 786440 | tf_op jit(solution)/shard_map/while/body/eval_jaxpr/ppermute | solution.py:29
  309.9 6.2 %collective-permute-start.2 = (f32[1,2,256,128]{3,2,1,0:T(8,128)S(1)}, f32[1,2,256,128]{3,2,1,0:T(8,128)S(1)}, u32[]{:S(2)}, u32[]{:S(2)}) collective-permute-start(f32[1,2,256,128]{3,2,1,0:T(8,128)S(1)} %get-tuple-element.485), channel_id=1, source_target_pairs={{0,4},{4,8},{8,12},{1,5},{5,9},{9,13},{2,6},{6,10},{10,14},{3,7},{... | collective-permute-start | bytes 786440 | tf_op jit(solution)/shard_map/while/body/eval_jaxpr/ppermute | solution.py:28
  312.2 8.3 %collective-permute-start.3 = (f32[1,2,256,128]{3,2,1,0:T(8,128)S(1)}, f32[1,2,256,128]{3,2,1,0:T(8,128)S(1)}, u32[]{:S(2)}, u32[]{:S(2)}) collective-permute-start(f32[1,2,256,128]{3,2,1,0:T(8,128)S(1)} %get-tuple-element.487), channel_id=1, source_target_pairs={{4,0},{8,4},{12,8},{5,1},{9,5},{13,9},{6,2},{10,6},{14,10},{7,3},{... | collective-permute-start | bytes 786440 | tf_op jit(solution)/shard_map/while/body/eval_jaxpr/ppermute | solution.py:29
  326.4 6.1 %collective-permute-start.2 = (f32[1,2,256,128]{3,2,1,0:T(8,128)S(1)}, f32[1,2,256,128]{3,2,1,0:T(8,128)S(1)}, u32[]{:S(2)}, u32[]{:S(2)}) collective-permute-start(f32[1,2,256,128]{3,2,1,0:T(8,128)S(1)} %get-tuple-element.485), channel_id=1, source_target_pairs={{0,4},{4,8},{8,12},{1,5},{5,9},{9,13},{2,6},{6,10},{10,14},{3,7},{... | collective-permute-start | bytes 786440 | tf_op jit(solution)/shard_map/while/body/eval_jaxpr/ppermute | solution.py:28
  328.7 8.3 %collective-permute-start.3 = (f32[1,2,256,128]{3,2,1,0:T(8,128)S(1)}, f32[1,2,256,128]{3,2,1,0:T(8,128)S(1)}, u32[]{:S(2)}, u32[]{:S(2)}) collective-permute-start(f32[1,2,256,128]{3,2,1,0:T(8,128)S(1)} %get-tuple-element.487), channel_id=1, source_target_pairs={{4,0},{8,4},{12,8},{5,1},{9,5},{13,9},{6,2},{10,6},{14,10},{7,3},{... | collective-permute-start | bytes 786440 | tf_op jit(solution)/shard_map/while/body/eval_jaxpr/ppermute | solution.py:29
  342.9 5.8 %collective-permute-start.2 = (f32[1,2,256,128]{3,2,1,0:T(8,128)S(1)}, f32[1,2,256,128]{3,2,1,0:T(8,128)S(1)}, u32[]{:S(2)}, u32[]{:S(2)}) collective-permute-start(f32[1,2,256,128]{3,2,1,0:T(8,128)S(1)} %get-tuple-element.485), channel_id=1, source_target_pairs={{0,4},{4,8},{8,12},{1,5},{5,9},{9,13},{2,6},{6,10},{10,14},{3,7},{... | collective-permute-start | bytes 786440 | tf_op jit(solution)/shard_map/while/body/eval_jaxpr/ppermute | solution.py:28
  344.9 8.3 %collective-permute-start.3 = (f32[1,2,256,128]{3,2,1,0:T(8,128)S(1)}, f32[1,2,256,128]{3,2,1,0:T(8,128)S(1)}, u32[]{:S(2)}, u32[]{:S(2)}) collective-permute-start(f32[1,2,256,128]{3,2,1,0:T(8,128)S(1)} %get-tuple-element.487), channel_id=1, source_target_pairs={{4,0},{8,4},{12,8},{5,1},{9,5},{13,9},{6,2},{10,6},{14,10},{7,3},{... | collective-permute-start | bytes 786440 | tf_op jit(solution)/shard_map/while/body/eval_jaxpr/ppermute | solution.py:29
  359.1 5.8 %collective-permute-start.2 = (f32[1,2,256,128]{3,2,1,0:T(8,128)S(1)}, f32[1,2,256,128]{3,2,1,0:T(8,128)S(1)}, u32[]{:S(2)}, u32[]{:S(2)}) collective-permute-start(f32[1,2,256,128]{3,2,1,0:T(8,128)S(1)} %get-tuple-element.485), channel_id=1, source_target_pairs={{0,4},{4,8},{8,12},{1,5},{5,9},{9,13},{2,6},{6,10},{10,14},{3,7},{... | collective-permute-start | bytes 786440 | tf_op jit(solution)/shard_map/while/body/eval_jaxpr/ppermute | solution.py:28
  361.1 8.3 %collective-permute-start.3 = (f32[1,2,256,128]{3,2,1,0:T(8,128)S(1)}, f32[1,2,256,128]{3,2,1,0:T(8,128)S(1)}, u32[]{:S(2)}, u32[]{:S(2)}) collective-permute-start(f32[1,2,256,128]{3,2,1,0:T(8,128)S(1)} %get-tuple-element.487), channel_id=1, source_target_pairs={{4,0},{8,4},{12,8},{5,1},{9,5},{13,9},{6,2},{10,6},{14,10},{7,3},{... | collective-permute-start | bytes 786440 | tf_op jit(solution)/shard_map/while/body/eval_jaxpr/ppermute | solution.py:29
  375.3 5.8 %collective-permute-start.2 = (f32[1,2,256,128]{3,2,1,0:T(8,128)S(1)}, f32[1,2,256,128]{3,2,1,0:T(8,128)S(1)}, u32[]{:S(2)}, u32[]{:S(2)}) collective-permute-start(f32[1,2,256,128]{3,2,1,0:T(8,128)S(1)} %get-tuple-element.485), channel_id=1, source_target_pairs={{0,4},{4,8},{8,12},{1,5},{5,9},{9,13},{2,6},{6,10},{10,14},{3,7},{... | collective-permute-start | bytes 786440 | tf_op jit(solution)/shard_map/while/body/eval_jaxpr/ppermute | solution.py:28
  377.3 8.3 %collective-permute-start.3 = (f32[1,2,256,128]{3,2,1,0:T(8,128)S(1)}, f32[1,2,256,128]{3,2,1,0:T(8,128)S(1)}, u32[]{:S(2)}, u32[]{:S(2)}) collective-permute-start(f32[1,2,256,128]{3,2,1,0:T(8,128)S(1)} %get-tuple-element.487), channel_id=1, source_target_pairs={{4,0},{8,4},{12,8},{5,1},{9,5},{13,9},{6,2},{10,6},{14,10},{7,3},{... | collective-permute-start | bytes 786440 | tf_op jit(solution)/shard_map/while/body/eval_jaxpr/ppermute | solution.py:29
  391.5 5.8 %collective-permute-start.2 = (f32[1,2,256,128]{3,2,1,0:T(8,128)S(1)}, f32[1,2,256,128]{3,2,1,0:T(8,128)S(1)}, u32[]{:S(2)}, u32[]{:S(2)}) collective-permute-start(f32[1,2,256,128]{3,2,1,0:T(8,128)S(1)} %get-tuple-element.485), channel_id=1, source_target_pairs={{0,4},{4,8},{8,12},{1,5},{5,9},{9,13},{2,6},{6,10},{10,14},{3,7},{... | collective-permute-start | bytes 786440 | tf_op jit(solution)/shard_map/while/body/eval_jaxpr/ppermute | solution.py:28
  393.5 8.3 %collective-permute-start.3 = (f32[1,2,256,128]{3,2,1,0:T(8,128)S(1)}, f32[1,2,256,128]{3,2,1,0:T(8,128)S(1)}, u32[]{:S(2)}, u32[]{:S(2)}) collective-permute-start(f32[1,2,256,128]{3,2,1,0:T(8,128)S(1)} %get-tuple-element.487), channel_id=1, source_target_pairs={{4,0},{8,4},{12,8},{5,1},{9,5},{13,9},{6,2},{10,6},{14,10},{7,3},{... | collective-permute-start | bytes 786440 | tf_op jit(solution)/shard_map/while/body/eval_jaxpr/ppermute | solution.py:29
  407.7 5.8 %collective-permute-start.2 = (f32[1,2,256,128]{3,2,1,0:T(8,128)S(1)}, f32[1,2,256,128]{3,2,1,0:T(8,128)S(1)}, u32[]{:S(2)}, u32[]{:S(2)}) collective-permute-start(f32[1,2,256,128]{3,2,1,0:T(8,128)S(1)} %get-tuple-element.485), channel_id=1, source_target_pairs={{0,4},{4,8},{8,12},{1,5},{5,9},{9,13},{2,6},{6,10},{10,14},{3,7},{... | collective-permute-start | bytes 786440 | tf_op jit(solution)/shard_map/while/body/eval_jaxpr/ppermute | solution.py:28
  409.7 8.3 %collective-permute-start.3 = (f32[1,2,256,128]{3,2,1,0:T(8,128)S(1)}, f32[1,2,256,128]{3,2,1,0:T(8,128)S(1)}, u32[]{:S(2)}, u32[]{:S(2)}) collective-permute-start(f32[1,2,256,128]{3,2,1,0:T(8,128)S(1)} %get-tuple-element.487), channel_id=1, source_target_pairs={{4,0},{8,4},{12,8},{5,1},{9,5},{13,9},{6,2},{10,6},{14,10},{7,3},{... | collective-permute-start | bytes 786440 | tf_op jit(solution)/shard_map/while/body/eval_jaxpr/ppermute | solution.py:29
  423.9 5.8 %collective-permute-start.2 = (f32[1,2,256,128]{3,2,1,0:T(8,128)S(1)}, f32[1,2,256,128]{3,2,1,0:T(8,128)S(1)}, u32[]{:S(2)}, u32[]{:S(2)}) collective-permute-start(f32[1,2,256,128]{3,2,1,0:T(8,128)S(1)} %get-tuple-element.485), channel_id=1, source_target_pairs={{0,4},{4,8},{8,12},{1,5},{5,9},{9,13},{2,6},{6,10},{10,14},{3,7},{... | collective-permute-start | bytes 786440 | tf_op jit(solution)/shard_map/while/body/eval_jaxpr/ppermute | solution.py:28
  425.9 8.3 %collective-permute-start.3 = (f32[1,2,256,128]{3,2,1,0:T(8,128)S(1)}, f32[1,2,256,128]{3,2,1,0:T(8,128)S(1)}, u32[]{:S(2)}, u32[]{:S(2)}) collective-permute-start(f32[1,2,256,128]{3,2,1,0:T(8,128)S(1)} %get-tuple-element.487), channel_id=1, source_target_pairs={{4,0},{8,4},{12,8},{5,1},{9,5},{13,9},{6,2},{10,6},{14,10},{7,3},{... | collective-permute-start | bytes 786440 | tf_op jit(solution)/shard_map/while/body/eval_jaxpr/ppermute | solution.py:29
  489.6 6.9 %collective-permute-start.4 = (f32[1,256,128]{2,1,0:T(8,128)S(1)}, f32[1,256,128]{2,1,0:T(8,128)S(1)}, u32[]{:S(2)}, u32[]{:S(2)}) collective-permute-start(f32[1,256,128]{2,1,0:T(8,128)S(1)} %slice.548), channel_id=1, source_target_pairs={{4,0},{8,4},{12,8},{5,1},{9,5},{13,9},{6,2},{10,6},{14,10},{7,3},{... | collective-permute-start | bytes 393224 | tf_op jit(solution)/shard_map/ppermute | solution.py:37
  496.9 4.0 collective-permute-start.5
  501.3 7.3 %collective-permute-start.6 = (f32[1,256,128]{2,1,0:T(8,128)S(1)}, f32[1,256,128]{2,1,0:T(8,128)S(1)}, u32[]{:S(2)}, u32[]{:S(2)}) collective-permute-start(f32[1,256,128]{2,1,0:T(8,128)S(1)} %slice.556), channel_id=1, source_target_pairs={{4,0},{8,4},{12,8},{5,1},{9,5},{13,9},{6,2},{10,6},{14,10},{7,3},{... | collective-permute-start | bytes 393224 | tf_op jit(solution)/shard_map/ppermute | solution.py:37
  509.0 6.4 %collective-permute-start.7 = (f32[1,256,128]{2,1,0:T(8,128)S(1)}, f32[1,256,128]{2,1,0:T(8,128)S(1)}, u32[]{:S(2)}, u32[]{:S(2)}) collective-permute-start(f32[1,256,128]{2,1,0:T(8,128)S(1)} %slice.557), channel_id=1, source_target_pairs={{0,4},{4,8},{8,12},{1,5},{5,9},{9,13},{2,6},{6,10},{10,14},{3,7},{... | collective-permute-start | bytes 393224 | tf_op jit(solution)/shard_map/ppermute | solution.py:37
  515.8 7.3 %collective-permute-start.8 = (f32[1,256,128]{2,1,0:T(8,128)S(1)}, f32[1,256,128]{2,1,0:T(8,128)S(1)}, u32[]{:S(2)}, u32[]{:S(2)}) collective-permute-start(f32[1,256,128]{2,1,0:T(8,128)S(1)} %slice.564), channel_id=1, source_target_pairs={{4,0},{8,4},{12,8},{5,1},{9,5},{13,9},{6,2},{10,6},{14,10},{7,3},{... | collective-permute-start | bytes 393224 | tf_op jit(solution)/shard_map/ppermute | solution.py:37
  523.4 6.4 %collective-permute-start.9 = (f32[1,256,128]{2,1,0:T(8,128)S(1)}, f32[1,256,128]{2,1,0:T(8,128)S(1)}, u32[]{:S(2)}, u32[]{:S(2)}) collective-permute-start(f32[1,256,128]{2,1,0:T(8,128)S(1)} %slice.565), channel_id=1, source_target_pairs={{0,4},{4,8},{8,12},{1,5},{5,9},{9,13},{2,6},{6,10},{10,14},{3,7},{... | collective-permute-start | bytes 393224 | tf_op jit(solution)/shard_map/ppermute | solution.py:37
  530.3 7.3 %collective-permute-start.10 = (f32[1,256,128]{2,1,0:T(8,128)S(1)}, f32[1,256,128]{2,1,0:T(8,128)S(1)}, u32[]{:S(2)}, u32[]{:S(2)}) collective-permute-start(f32[1,256,128]{2,1,0:T(8,128)S(1)} %slice.572), channel_id=1, source_target_pairs={{4,0},{8,4},{12,8},{5,1},{9,5},{13,9},{6,2},{10,6},{14,10},{7,3},{... | collective-permute-start | bytes 393224 | tf_op jit(solution)/shard_map/ppermute | solution.py:37
  537.9 6.9 %collective-permute-start.11 = (f32[1,256,128]{2,1,0:T(8,128)S(1)}, f32[1,256,128]{2,1,0:T(8,128)S(1)}, u32[]{:S(2)}, u32[]{:S(2)}) collective-permute-start(f32[1,256,128]{2,1,0:T(8,128)S(1)} %slice.573), channel_id=1, source_target_pairs={{0,4},{4,8},{8,12},{1,5},{5,9},{9,13},{2,6},{6,10},{10,14},{3,7},{... | collective-permute-start | bytes 393224 | tf_op jit(solution)/shard_map/ppermute | solution.py:37
  545.2 8.7 %collective-permute-start.12 = (f32[1,256,128]{2,1,0:T(8,128)S(1)}, f32[1,256,128]{2,1,0:T(8,128)S(1)}, u32[]{:S(2)}, u32[]{:S(2)}) collective-permute-start(f32[1,256,128]{2,1,0:T(8,128)S(1)} %slice.580), channel_id=1, source_target_pairs={{4,0},{8,4},{12,8},{5,1},{9,5},{13,9},{6,2},{10,6},{14,10},{7,3},{... | collective-permute-start | bytes 393224 | tf_op jit(solution)/shard_map/ppermute | solution.py:37
  554.2 6.6 %collective-permute-start.13 = (f32[1,256,128]{2,1,0:T(8,128)S(1)}, f32[1,256,128]{2,1,0:T(8,128)S(1)}, u32[]{:S(2)}, u32[]{:S(2)}) collective-permute-start(f32[1,256,128]{2,1,0:T(8,128)S(1)} %slice.581), channel_id=1, source_target_pairs={{0,4},{4,8},{8,12},{1,5},{5,9},{9,13},{2,6},{6,10},{10,14},{3,7},{... | collective-permute-start | bytes 393224 | tf_op jit(solution)/shard_map/ppermute | solution.py:37
  561.2 7.3 %collective-permute-start.14 = (f32[1,256,128]{2,1,0:T(8,128)S(1)}, f32[1,256,128]{2,1,0:T(8,128)S(1)}, u32[]{:S(2)}, u32[]{:S(2)}) collective-permute-start(f32[1,256,128]{2,1,0:T(8,128)S(1)} %slice.588), channel_id=1, source_target_pairs={{4,0},{8,4},{12,8},{5,1},{9,5},{13,9},{6,2},{10,6},{14,10},{7,3},{... | collective-permute-start | bytes 393224 | tf_op jit(solution)/shard_map/ppermute | solution.py:37
  568.9 6.4 %collective-permute-start.15 = (f32[1,256,128]{2,1,0:T(8,128)S(1)}, f32[1,256,128]{2,1,0:T(8,128)S(1)}, u32[]{:S(2)}, u32[]{:S(2)}) collective-permute-start(f32[1,256,128]{2,1,0:T(8,128)S(1)} %slice.589), channel_id=1, source_target_pairs={{0,4},{4,8},{8,12},{1,5},{5,9},{9,13},{2,6},{6,10},{10,14},{3,7},{... | collective-permute-start | bytes 393224 | tf_op jit(solution)/shard_map/ppermute | solution.py:37
  (12 other events, 127.5 us)
Sparse Core Ops, SparseCore 0:
  441.0 32.5 all-reduce.29
where the time goes:
time: 586 us; the launch traced here: 583 us
  waiting for transfers between devices  244 us (42%)
  other arithmetic  136 us (23%)
  starting transfers between devices  115 us (20%)
  local copies, waits for them, and re-layouts  58.2 us (10%)
  between operations  15.2 us (3%)
  blocking collectives  12.3 us (2%)
    ppermute x24, waiting for transfers between devices, padded_2(): after = lax.ppermute(initial, axis, down)  102 us
    scatter-add x48, other arithmetic, per_device(): flat_field.at[slots].add(amounts)  70.8 us
    ppermute x24, waiting for transfers between devices, padded_2(): before = lax.ppermute(last, axis, up)  59.6 us
    ppermute x24, starting transfers between devices, padded_2(): before = lax.ppermute(last, axis, up)  55.3 us
    ppermute x12, waiting for transfers between devices, from_behind(): lax.ppermute(value, axis, [(source, source + steps) for source in range(i...  49.1 us
    gather x24, local copies, waits for them, and re-layouts, per_device(): sample_at = jax.vmap(lambda flat_field, slots: flat_field[slots])  42.1 us
    psum x1, waiting for transfers between devices, per_device(): slab_gradient = lax.psum(local_gradient, 'shot')  32.7 us
    ppermute x24, starting transfers between devices, padded_2(): after = lax.ppermute(initial, axis, down)  31 us
  transfers between devices with their start and end apart: 61, of which 61 were waited for; matrix products, arithmetic and copies ran while one was open for 2% of the time, Pallas kernels for 0%

commit v1 on v0

v1 whole, which is shorter than its diff:
```python
import functools

import jax
import jax.numpy as jnp
from jax import lax
from jax.experimental import pallas as pl
from jax.experimental.pallas import tpu as pltpu
from jax.sharding import PartitionSpec as P

ITERS = 6

near_weight = 4.0 / 3.0
far_weight = -1.0 / 12.0
centre_weight = 7.5
step_length = 0.02
tv_bound = 0.01
dual_step = 0.25
primal_step = 0.25
lower_bound = 0.08
upper_bound = 0.22
epsilon = 1e-06

VMEM_LIMIT = 58 * 1024 * 1024


def from_behind(value, axis, steps):
    count = lax.axis_size(axis)
    initial, last = (max(0, -steps), min(count, count - steps))
    return lax.ppermute(value, axis, [(source, source + steps) for source in range(initial, last)])


def forward_part(field, along, upper, last_owner):
    size = field.shape[along]
    first_row = lax.slice_in_dim(field, 0, 1, axis=along)
    remainder = lax.slice_in_dim(field, 1, size, axis=along)
    beyond = jnp.zeros_like(first_row) if upper is None else upper(first_row)
    difference = jnp.concatenate([remainder, beyond], along) - field
    row_index = lax.broadcasted_iota(jnp.int32, field.shape, along)
    return jnp.where(jnp.logical_and(row_index == size - 1, last_owner), 0.0, difference)


def backward_part(dual, along, lower):
    size = dual.shape[along]
    last_row = lax.slice_in_dim(dual, size - 1, size, axis=along)
    before = jnp.zeros_like(last_row) if lower is None else lower(last_row)
    earlier = jnp.concatenate([before, lax.slice_in_dim(dual, 0, size - 1, axis=along)], along)
    return earlier - dual


def project(target, upper_x, lower_x, last_x):
    field = jnp.clip(target, lower_bound, upper_bound)
    extrap = field
    duals = [jnp.zeros_like(field) for along in range(3)]
    for iteration in range(ITERS):
        duals = [
            jnp.clip(
                duals[0] + dual_step * forward_part(extrap, 0, upper_x, last_x), -tv_bound, tv_bound
            ),
            jnp.clip(
                duals[1] + dual_step * forward_part(extrap, 1, None, True), -tv_bound, tv_bound
            ),
            jnp.clip(
                duals[2] + dual_step * forward_part(extrap, 2, None, True), -tv_bound, tv_bound
            ),
        ]
        adjoint = (
            backward_part(duals[0], 0, lower_x)
            + backward_part(duals[1], 1, None)
            + backward_part(duals[2], 2, None)
        )
        following = jnp.clip(
            (field - primal_step * adjoint + primal_step * target) / (1.0 + primal_step),
            lower_bound,
            upper_bound,
        )
        extrap = 2.0 * following - field
        field = following
    return field


def two_pieces(value):
    high = value.astype(jnp.bfloat16)
    low = (value - high.astype(jnp.float32)).astype(jnp.bfloat16)
    return high, low


def one_hot_rows(cells, layers, rows, first_row, height, width):
    lines = cells // width
    layer = lines // height
    row = lines - layer * height - first_row
    inside = jnp.logical_and(row >= 0, row < rows)
    return jnp.where(inside, layer * rows + row, -1)


def advance(model, current, earlier, injected, column, extent, keep, accumulate):
    layers, rows, width = extent
    lane = lax.broadcasted_iota(jnp.int32, (1, width), 1)
    weights = [
        (1, jnp.where(lane >= 1, near_weight, 0.0)),
        (width - 1, jnp.where(lane < width - 1, near_weight, 0.0)),
        (2, jnp.where(lane >= 2, far_weight, 0.0)),
        (width - 2, jnp.where(lane < width - 2, far_weight, 0.0)),
    ]

    def layer_step(layer, carry):
        centre = current[layer + 2]
        near = current[layer + 1] + current[layer + 3]
        far = current[layer] + current[layer + 4]
        near = near + (pltpu.roll(centre, 1, 0) + pltpu.roll(centre, rows - 1, 0))
        far = far + (pltpu.roll(centre, 2, 0) + pltpu.roll(centre, rows - 2, 0))
        lap = near_weight * near + far_weight * far - centre_weight * centre
        for shift, weight in weights:
            lap = lap + weight * pltpu.roll(centre, shift, 1)
        start = layer * rows if isinstance(layer, int) else pl.multiple_of(layer * rows, 8)
        following = 2.0 * centre - earlier[layer + 2] + model[layer] * lap
        following = following + injected[pl.ds(start, rows), pl.ds(column, width)]
        earlier[layer + 2] = following
        if keep is not None:
            keep(layer, lap)
        if accumulate is not None:
            accumulate(layer, following)
        return carry

    if layers <= 16:
        for layer in range(layers):
            layer_step(layer, 0)
    else:
        lax.fori_loop(0, layers, layer_step, 0)


def fill_one_hot(target, positions):
    step = 256
    for begin in range(0, target.shape[0], step):
        grid_row = lax.broadcasted_iota(jnp.int32, (step, target.shape[1]), 0) + begin
        target[begin : begin + step, :] = jnp.where(grid_row == positions, 1.0, 0.0).astype(jnp.bfloat16)


def inject(spread, values, injected):
    high, low = two_pieces(values)
    injected[...] = jnp.dot(spread[...], high, preferred_element_type=jnp.float32) + jnp.dot(
        spread[...], low, preferred_element_type=jnp.float32
    )


def forward_kernel(
    geometry, model, sources, receivers_column, values, laps, record, first, second, injected, spread, pick
):
    layers, rows, own, halo, height, width = geometry
    start_row = lax.axis_index("sub") * own
    fill_one_hot(spread, one_hot_rows(sources[...], layers, rows, start_row - halo, height, width))
    first[...] = jnp.zeros_like(first)
    second[...] = jnp.zeros_like(second)
    column = receivers_column[...]
    owned = one_hot_rows(column, layers, own, start_row, height, width)
    cells = layers * own
    for begin in range(0, cells, 256):
        numbers = lax.broadcasted_iota(jnp.int32, (column.shape[0], 256), 1) + begin
        pick[:, begin : begin + 256] = jnp.where(numbers == owned, 1.0, 0.0).astype(jnp.bfloat16)
    lane = lax.broadcasted_iota(jnp.int32, (column.shape[0], width), 1)
    mask = jnp.where(lane == column - (column // width) * width, 1.0, 0.0)
    ones = jnp.ones((8, width), jnp.bfloat16)

    def sample(field, step):
        values = field[2 : 2 + layers, halo : halo + own, :].reshape(cells, width)
        found = [
            jnp.dot(pick[...], piece, preferred_element_type=jnp.float32)
            for piece in two_pieces(values)
        ]
        pieces = [piece * mask for piece in found]
        total = jnp.zeros((8, column.shape[0]), jnp.float32)
        for piece in pieces:
            total = total + lax.dot_general(
                ones, piece.astype(jnp.bfloat16), (((1,), (1,)), ((), ())), preferred_element_type=jnp.float32
            )
        record[pl.ds(step, 1), :] = total[0:1]

    def pair(number, carry):
        inject(spread, values[number], injected)
        for half, (current, earlier) in enumerate(((second, first), (first, second))):
            step = number * 2 + half

            def keep(layer, lap):
                laps[step, layer] = lap[halo : halo + own]

            advance(model, current, earlier, injected, half * width, (layers, rows, width), keep, None)
            sample(earlier, step)
        return carry

    lax.fori_loop(0, values.shape[0], pair, 0)


def backward_kernel(geometry, model, receivers, values, laps, gradient, first, second, injected, spread):
    layers, rows, own, halo, height, width = geometry
    start_row = lax.axis_index("sub") * own
    fill_one_hot(spread, one_hot_rows(receivers[...], layers, rows, start_row - halo, height, width))
    first[...] = jnp.zeros_like(first)
    second[...] = jnp.zeros_like(second)
    gradient[...] = jnp.zeros_like(gradient)
    steps = laps.shape[0]

    def pair(number, carry):
        inject(spread, values[number], injected)
        for half, (current, earlier) in enumerate(((second, first), (first, second))):
            step = number * 2 + half

            def accumulate(layer, following):
                gradient[layer] += following[halo : halo + own] * laps[steps - 1 - step, layer]

            advance(
                model, current, earlier, injected, half * width, (layers, rows, width), None, accumulate
            )
        return carry

    lax.fori_loop(0, values.shape[0], pair, 0)


def spread_values(amounts, cells, width):
    steps, points = amounts.shape
    pairs = amounts.reshape(steps // 2, 2, points)
    lane = cells % width
    hot = (lane[:, None] == jnp.arange(width, dtype=jnp.int32)[None]).astype(jnp.float32)
    spread = [pairs[:, half, :, None] * hot[None] for half in range(2)]
    return jnp.concatenate(spread, axis=2)


def per_device(model_field, source_index, wavelets, receiver_index, observed):
    slab, height, width = model_field.shape
    subs = lax.axis_size("sub")
    layers = slab * subs
    own = height // subs
    steps = wavelets.shape[1]
    halo = 2 * steps
    rows = own + 2 * halo
    geometry = (layers, rows, own, halo, height, width)

    wide = jnp.pad(model_field, ((0, 0), (halo, halo), (0, 0)))
    parts = jnp.stack([wide[:, j * own : j * own + rows] for j in range(subs)])
    model = lax.all_to_all(parts, "sub", 0, 0).reshape(layers, rows, width)

    vmem = pl.BlockSpec(memory_space=pltpu.VMEM)
    field = pltpu.VMEM((layers + 4, rows, width), jnp.float32)
    injected = pltpu.VMEM((layers * rows, 2 * width), jnp.float32)
    params = pltpu.CompilerParams(vmem_limit_bytes=VMEM_LIMIT)
    sources, receivers = source_index, receiver_index
    values = spread_values(wavelets[0], sources[0], width)
    laps, record = pl.pallas_call(
        functools.partial(forward_kernel, geometry),
        out_shape=(
            jax.ShapeDtypeStruct((steps, layers, own, width), jnp.float32),
            jax.ShapeDtypeStruct((steps, receivers.shape[1]), jnp.float32),
        ),
        in_specs=[vmem] * 4,
        out_specs=(vmem, vmem),
        scratch_shapes=[
            field,
            field,
            injected,
            pltpu.VMEM((layers * rows, sources.shape[1]), jnp.bfloat16),
            pltpu.VMEM((receivers.shape[1], layers * own), jnp.bfloat16),
        ],
        compiler_params=params,
    )(model, sources, receivers.reshape(-1, 1), values)
    misfit = lax.psum(record, "sub") - observed[0]
    values = spread_values(misfit[::-1], receivers[0], width)
    part_gradient = pl.pallas_call(
        functools.partial(backward_kernel, geometry),
        out_shape=jax.ShapeDtypeStruct((layers, own, width), jnp.float32),
        in_specs=[vmem] * 4,
        out_specs=vmem,
        scratch_shapes=[
            field,
            field,
            injected,
            pltpu.VMEM((layers * rows, receivers.shape[1]), jnp.bfloat16),
        ],
        compiler_params=params,
    )(model, receivers, values, laps)

    local_gradient = lax.all_to_all(part_gradient.reshape(subs, slab, own, width), "sub", 0, 0)
    local_gradient = jnp.swapaxes(local_gradient, 0, 1).reshape(slab, height, width)
    last_x = lax.axis_index("sub") == subs - 1
    slab_gradient = lax.psum(local_gradient, "shot")
    square_sum = lax.psum(jnp.sum(slab_gradient * slab_gradient), "sub")
    grad_scale = jnp.sqrt(square_sum / (slab * height * width * subs) + epsilon)
    target = model_field - step_length * (slab_gradient / grad_scale)

    def slab_upper(layer):
        return from_behind(layer, "sub", -1)

    def slab_lower(layer):
        return from_behind(layer, "sub", 1)

    updated_model = project(target, slab_upper, slab_lower, last_x)
    brick_rows = height // lax.axis_size("shot")
    gradient = lax.dynamic_slice_in_dim(
        slab_gradient, lax.axis_index("shot") * brick_rows, brick_rows, 1
    )
    return (updated_model, gradient)


def solution(mesh):
    placed = (
        P(("grp", "sub"), None, None),
        P(("grp", "shot"), None),
        P(("grp", "shot"), None, None),
        P(("grp", "shot"), None),
        P(("grp", "shot"), None, None),
    )
    return jax.shard_map(
        per_device,
        mesh=mesh,
        in_specs=placed,
        out_specs=(P(("grp", "sub"), None, None), P(("grp", "sub"), "shot", None)),
        check_vma=False,
    )
```

time: 586 us -> 262 us (0.45)
  waiting for transfers between devices: 244 us -> 101 us
  other arithmetic: 136 us -> 13.9 us
  starting transfers between devices: 115 us -> 35.2 us
  local copies, waits for them, and re-layouts: 58.2 us -> 7.61 us
  Pallas kernels: 0 us -> 44.3 us
  blocking collectives: 12.3 us -> 43.9 us
    ppermute x48 -> x0, waiting for transfers between devices: 162 us -> none  [the longest x24 102 us: padded_2(): after = lax.ppermute(initial, axis, down)]
    ppermute x48 -> x0, starting transfers between devices: 86.3 us -> none  [the longest x24 55.3 us: padded_2(): before = lax.ppermute(last, axis, up)]
    scatter-add x48 -> x0, other arithmetic: 70.8 us -> none  [per_device(): flat_field.at[slots].add(amounts)]
    pallas_call x0 -> x2, Pallas kernels: none -> 44.3 us  [the longest x1 23.7 us: per_device(): pl.pallas_call(functools.partial(forward_kernel, geometry), out_shape=(ja...]
    gather x24 -> x0, local copies, waits for them, and re-layouts: 42.1 us -> none  [per_device(): sample_at = jax.vmap(lambda flat_field, slots: flat_field[slots])]
    all_to_all x0 -> x1, waiting for transfers between devices: none -> 20 us  [per_device(): model = lax.all_to_all(parts, 'sub', 0, 0).reshape(layers, rows, width)]
    add x36 -> x0, other arithmetic: 19.9 us -> none  [the longest x12 16.4 us: backward(): return ((current, following, gradient_sum + following * stored), None)]
    psum x0 -> x1, blocking collectives: none -> 17.7 us  [per_device(): misfit = lax.psum(record, 'sub') - observed[0]]
  transfers between devices with their start and end apart: 61 -> 14, of which waited for: 61 -> 14; matrix products, arithmetic and copies ran while one was open for 2% -> 2% of each run, Pallas kernels for 0% -> 0%
where the time goes in v1:
time: 262 us; the launch traced here: 261 us
  waiting for transfers between devices  101 us (39%)
  Pallas kernels  44.3 us (17%)
  blocking collectives  43.9 us (17%)
  starting transfers between devices  35.2 us (13%)
  between operations  15.3 us (6%)
  other arithmetic  13.9 us (5%)
  local copies, waits for them, and re-layouts  7.61 us (3%)
    ppermute x12, waiting for transfers between devices, from_behind(): lax.ppermute(value, axis, [(source, source + steps) for source in range(i...  49 us
    psum x1, waiting for transfers between devices, per_device(): slab_gradient = lax.psum(local_gradient, 'shot')  32.3 us
    ppermute x12, starting transfers between devices, from_behind(): lax.ppermute(value, axis, [(source, source + steps) for source in range(i...  28.9 us
    pallas_call x1, Pallas kernels, per_device(): pl.pallas_call(functools.partial(forward_kernel, geometry), out_shape=(ja...  23.7 us
    pallas_call x1, Pallas kernels, per_device(): pl.pallas_call(functools.partial(backward_kernel, geometry), out_shape=ja...  20.6 us
    all_to_all x1, waiting for transfers between devices, per_device(): model = lax.all_to_all(parts, 'sub', 0, 0).reshape(layers, rows, width)  20 us
    psum x1, blocking collectives, per_device(): misfit = lax.psum(record, 'sub') - observed[0]  17.7 us
    all_to_all x1, blocking collectives, per_device(): lax.all_to_all(part_gradient.reshape(subs, slab, own, width), 'sub', 0, 0)  13.9 us
  transfers between devices with their start and end apart: 14, of which 14 were waited for; matrix products, arithmetic and copies ran while one was open for 2% of the time, Pallas kernels for 0%

profile of v1, /device:TPU:0, one launch (start us, length us, event | category | flops | bytes accessed | tf_op | source)
XLA Modules:
  0.0 261.5 jit_solution(5854369591148336295)
XLA Ops:
  7.2 1.3 fusion.66
  8.5 1.0 pad_maximum_fusion.2
  9.5 6.3 %all-to-all-start = ((f32[4,4,112,128]{3,2,1,0:T(8,128)}), f32[4,4,112,128]{3,2,1,0:T(8,128)S(1)}, u32[]{:S(2)}, u32[]{:S(2)}) async-start(f32[4,4,112,128]{3,2,1,0:T(8,128)} %pad_maximum_fusion.2), calls=%async_computation | async-start | bytes 1835008 | tf_op jit(solution)/shard_map/all_to_all | solution.py:238
  15.9 0.9 copy.14.receivers_column
  16.9 0.5 broadcast_multiply_fusion.3
  17.4 1.2 pad_maximum_fusion.1.values
  18.6 0.1 fusion.65
  18.8 20.0 %all-to-all-done = f32[4,4,112,128]{3,2,1,0:T(8,128)S(1)} async-done(((f32[4,4,112,128]{3,2,1,0:T(8,128)}), f32[4,4,112,128]{3,2,1,0:T(8,128)S(1)}, u32[]{:S(2)}, u32[]{:S(2)}) %all-to-all-start) | async-done | bytes 917536 | tf_op jit(solution)/shard_map/all_to_all | solution.py:238
  38.7 0.9 copy-done
  39.7 23.7 %shard_map.68 = (f32[12,16,64,128]{3,2,1,0:T(8,128)}, f32[12,512]{1,0:T(8,128)}) custom-call(f32[16,112,128]{2,1,0:T(8,128)} %bitcast.49, s32[1,256]{1,0:T(1,128)} %sources.1, s32[512,1]{1,0:T(8,128)} %copy.14.receivers_column, f32[6,256,256]{2,1,0:T(8,128)} %pad_maximum_fusion.1.values), custom_call_target="tpu_custom_call" | custom-call | tf_op jit(solution)/shard_map/pallas_call | solution.py:246
  63.4 17.7 %psum.21 = f32[12,512]{1,0:T(8,128)S(1)} all-reduce(f32[12,512]{1,0:T(8,128)} %get-tuple-element.4), channel_id=1, replica_groups=mesh['grp'=2,'sub'=4,'shot'=4] {'sub'}, use_global_device_ids=true, to_apply=%region_0.1 | all-reduce | flops 6144 | bytes 49152 | tf_op jit(solution)/shard_map/psum | solution.py:263
  81.2 0.1 rev.3
  81.4 0.9 broadcast_multiply_fusion.1
  82.3 1.9 pad_maximum_fusion.values
  84.2 20.6 %shard_map.69 = f32[16,64,128]{2,1,0:T(8,128)} custom-call(f32[16,112,128]{2,1,0:T(8,128)} %bitcast.50, s32[1,512]{1,0:T(1,128)} %receivers.1, f32[6,512,256]{2,1,0:T(8,128)} %pad_maximum_fusion.values, f32[12,16,64,128]{3,2,1,0:T(8,128)} %get-tuple-element.5.laps), custom_call_target="tpu_custom_call" | custom-call | tf_op jit(solution)/shard_map/pallas_call | solution.py:265
  104.8 13.9 %all_to_all.10 = f32[4,4,64,128]{3,2,1,0:T(8,128)S(1)} all-to-all(f32[4,4,64,128]{3,2,1,0:T(8,128)} %bitcast.53), channel_id=1, replica_groups=mesh['grp'=2,'sub'=4,'shot'=4] {'sub'}, dimensions={0} | all-to-all | bytes 1048576 | tf_op jit(solution)/shard_map/all_to_all | solution.py:279
  118.6 0.8 copy.17
  119.5 32.3 %all-reduce.27.cloned.1.call-done = f32[4,256,128]{2,1,0:T(8,128)} async-done(((f32[4,256,128]{2,1,0:T(8,128)}), f32[4,256,128]{2,1,0:T(8,128)}) %all-reduce.27.cloned.1.call-update) | async-done | bytes 524304 | tf_op jit(solution)/shard_map/psum | solution.py:282
  151.8 1.8 multiply_reduce_fusion
  153.6 12.3 %psum.23 = f32[]{:T(128)} all-reduce(f32[]{:T(128)} %multiply_reduce_fusion), channel_id=1, replica_groups=mesh['grp'=2,'sub'=4,'shot'=4] {'sub'}, use_global_device_ids=true, to_apply=%region_3.4 | all-reduce | flops 1 | bytes 8 | tf_op jit(solution)/shard_map/psum | solution.py:283
  166.6 1.2 broadcast_clamp_fusion
  167.8 1.3 collective-permute-start
  169.2 0.2 slice.236
  169.4 5.2 %collective-permute-done = f32[1,256,128]{2,1,0:T(8,128)S(1)} collective-permute-done((f32[1,256,128]{2,1,0:T(8,128)S(1)}, f32[1,256,128]{2,1,0:T(8,128)S(1)}, u32[]{:S(2)}, u32[]{:S(2)}) %collective-permute-start) | collective-permute-done | bytes 131104 | tf_op jit(solution)/shard_map/ppermute | solution.py:29
  174.7 0.3 fusion.2
  175.0 1.5 collective-permute-start.1
  176.6 2.5 collective-permute-done.1
  179.0 0.4 multiply_subtract_fusion.4
  179.4 1.5 collective-permute-start.2
  181.0 0.2 slice.244
  181.2 5.5 %collective-permute-done.2 = f32[1,256,128]{2,1,0:T(8,128)S(1)} collective-permute-done((f32[1,256,128]{2,1,0:T(8,128)S(1)}, f32[1,256,128]{2,1,0:T(8,128)S(1)}, u32[]{:S(2)}, u32[]{:S(2)}) %collective-permute-start.2) | collective-permute-done | bytes 131104 | tf_op jit(solution)/shard_map/ppermute | solution.py:29
  186.7 0.3 fusion.13
  187.1 3.9 %collective-permute-start.3 = (f32[1,256,128]{2,1,0:T(8,128)S(1)}, f32[1,256,128]{2,1,0:T(8,128)S(1)}, u32[]{:S(2)}, u32[]{:S(2)}) collective-permute-start(f32[1,256,128]{2,1,0:T(8,128)S(1)} %slice.240), channel_id=1, source_target_pairs={{0,4},{4,8},{8,12},{1,5},{5,9},{9,13},{2,6},{6,10},{10,14},{3,7},{... | collective-permute-start | bytes 393224 | tf_op jit(solution)/shard_map/ppermute | solution.py:29
  191.1 2.5 collective-permute-done.3
  193.5 0.4 multiply_subtract_fusion.3
  193.9 1.3 collective-permute-start.4
  195.3 0.2 slice.252
  195.5 5.7 %collective-permute-done.4 = f32[1,256,128]{2,1,0:T(8,128)S(1)} collective-permute-done((f32[1,256,128]{2,1,0:T(8,128)S(1)}, f32[1,256,128]{2,1,0:T(8,128)S(1)}, u32[]{:S(2)}, u32[]{:S(2)}) %collective-permute-start.4) | collective-permute-done | bytes 131104 | tf_op jit(solution)/shard_map/ppermute | solution.py:29
  201.2 0.3 fusion.24
  201.6 3.9 %collective-permute-start.5 = (f32[1,256,128]{2,1,0:T(8,128)S(1)}, f32[1,256,128]{2,1,0:T(8,128)S(1)}, u32[]{:S(2)}, u32[]{:S(2)}) collective-permute-start(f32[1,256,128]{2,1,0:T(8,128)S(1)} %slice.248), channel_id=1, source_target_pairs={{0,4},{4,8},{8,12},{1,5},{5,9},{9,13},{2,6},{6,10},{10,14},{3,7},{... | collective-permute-start | bytes 393224 | tf_op jit(solution)/shard_map/ppermute | solution.py:29
  205.6 2.5 collective-permute-done.5
  208.0 0.4 multiply_subtract_fusion.2
  208.4 1.3 collective-permute-start.6
  209.8 0.2 slice.260
  210.0 5.7 %collective-permute-done.6 = f32[1,256,128]{2,1,0:T(8,128)S(1)} collective-permute-done((f32[1,256,128]{2,1,0:T(8,128)S(1)}, f32[1,256,128]{2,1,0:T(8,128)S(1)}, u32[]{:S(2)}, u32[]{:S(2)}) %collective-permute-start.6) | collective-permute-done | bytes 131104 | tf_op jit(solution)/shard_map/ppermute | solution.py:29
  215.7 0.3 fusion.35
  216.1 3.9 %collective-permute-start.7 = (f32[1,256,128]{2,1,0:T(8,128)S(1)}, f32[1,256,128]{2,1,0:T(8,128)S(1)}, u32[]{:S(2)}, u32[]{:S(2)}) collective-permute-start(f32[1,256,128]{2,1,0:T(8,128)S(1)} %slice.256), channel_id=1, source_target_pairs={{0,4},{4,8},{8,12},{1,5},{5,9},{9,13},{2,6},{6,10},{10,14},{3,7},{... | collective-permute-start | bytes 393224 | tf_op jit(solution)/shard_map/ppermute | solution.py:29
  220.0 2.9 %collective-permute-done.7 = f32[1,256,128]{2,1,0:T(8,128)S(1)} collective-permute-done((f32[1,256,128]{2,1,0:T(8,128)S(1)}, f32[1,256,128]{2,1,0:T(8,128)S(1)}, u32[]{:S(2)}, u32[]{:S(2)}) %collective-permute-start.7) | collective-permute-done | bytes 131104 | tf_op jit(solution)/shard_map/ppermute | solution.py:29
  222.9 0.4 multiply_subtract_fusion.1
  223.3 1.3 collective-permute-start.8
  224.7 0.2 slice.268
  224.9 7.1 %collective-permute-done.8 = f32[1,256,128]{2,1,0:T(8,128)S(1)} collective-permute-done((f32[1,256,128]{2,1,0:T(8,128)S(1)}, f32[1,256,128]{2,1,0:T(8,128)S(1)}, u32[]{:S(2)}, u32[]{:S(2)}) %collective-permute-start.8) | collective-permute-done | bytes 131104 | tf_op jit(solution)/shard_map/ppermute | solution.py:29
  232.0 0.3 fusion.46
  232.4 3.8 %collective-permute-start.9 = (f32[1,256,128]{2,1,0:T(8,128)S(1)}, f32[1,256,128]{2,1,0:T(8,128)S(1)}, u32[]{:S(2)}, u32[]{:S(2)}) collective-permute-start(f32[1,256,128]{2,1,0:T(8,128)S(1)} %slice.264), channel_id=1, source_target_pairs={{0,4},{4,8},{8,12},{1,5},{5,9},{9,13},{2,6},{6,10},{10,14},{3,7},{... | collective-permute-start | bytes 393224 | tf_op jit(solution)/shard_map/ppermute | solution.py:29
  236.2 2.8 %collective-permute-done.9 = f32[1,256,128]{2,1,0:T(8,128)S(1)} collective-permute-done((f32[1,256,128]{2,1,0:T(8,128)S(1)}, f32[1,256,128]{2,1,0:T(8,128)S(1)}, u32[]{:S(2)}, u32[]{:S(2)}) %collective-permute-start.9) | collective-permute-done | bytes 131104 | tf_op jit(solution)/shard_map/ppermute | solution.py:29
  239.0 0.4 multiply_subtract_fusion
  239.4 1.3 collective-permute-start.10
  240.7 0.2 slice.276
  240.9 5.7 %collective-permute-done.10 = f32[1,256,128]{2,1,0:T(8,128)S(1)} collective-permute-done((f32[1,256,128]{2,1,0:T(8,128)S(1)}, f32[1,256,128]{2,1,0:T(8,128)S(1)}, u32[]{:S(2)}, u32[]{:S(2)}) %collective-permute-start.10) | collective-permute-done | bytes 131104 | tf_op jit(solution)/shard_map/ppermute | solution.py:29
  246.7 0.3 add_clamp_fusion.1
  247.1 3.9 %collective-permute-start.11 = (f32[1,256,128]{2,1,0:T(8,128)S(1)}, f32[1,256,128]{2,1,0:T(8,128)S(1)}, u32[]{:S(2)}, u32[]{:S(2)}) collective-permute-start(f32[1,256,128]{2,1,0:T(8,128)S(1)} %slice.272), channel_id=1, source_target_pairs={{0,4},{4,8},{8,12},{1,5},{5,9},{9,13},{2,6},{6,10},{10,14},{3,7},{... | collective-permute-start | bytes 393224 | tf_op jit(solution)/shard_map/ppermute | solution.py:29
  251.0 1.6 constant_dynamic-slice_fusion
  252.6 0.9 collective-permute-done.11
  253.5 1.1 fusion.64
  (58 shorter events, 1.0 us)
Async XLA Ops:
  8.5 7.4 %copy-start.4 = (f32[1,12,256]{2,0,1:T(1,128)S(1)}, f32[1,12,256]{2,0,1:T(1,128)}, u32[]{:S(2)}) copy-start(f32[1,12,256]{2,0,1:T(1,128)} %param.7) | copy-start | bytes 36868
  8.5 7.4 %copy-start.5 = (s32[1,256]{1,0:T(1,128)S(1)}, s32[1,256]{1,0:T(1,128)}, u32[]{:S(2)}) copy-start(s32[1,256]{1,0:T(1,128)} %sources.1) | copy-start | bytes 3076
  8.5 7.4 %copy-start.3 = (s32[1,512]{1,0:T(1,128)S(1)}, s32[1,512]{1,0:T(1,128)}, u32[]{:S(2)}) copy-start(s32[1,512]{1,0:T(1,128)} %receivers.1) | copy-start | bytes 6148
  9.5 29.2 %all-to-all-start = ((f32[4,4,112,128]{3,2,1,0:T(8,128)}), f32[4,4,112,128]{3,2,1,0:T(8,128)S(1)}, u32[]{:S(2)}, u32[]{:S(2)}) async-start(f32[4,4,112,128]{3,2,1,0:T(8,128)} %pad_maximum_fusion.2), calls=%async_computation | async-start | bytes 1835008 | tf_op jit(solution)/shard_map/all_to_all | solution.py:238
  15.8 136.0 %all-reduce.27.cloned.1.call-start = ((), (), s32[]{:S(2)}) async-start(), calls=%async_computation.2 | async-start | bytes 1048576 | tf_op jit(solution)/shard_map/psum | solution.py:282
  18.6 62.5 %copy-start.2 = (f32[1,12,512]{2,0,1:T(1,128)S(1)}, f32[1,12,512]{2,0,1:T(1,128)}, u32[]{:S(2)}) copy-start(f32[1,12,512]{2,0,1:T(1,128)} %param.9) | copy-start | bytes 73732
  38.7 0.9 copy-start
  104.8 61.8 %copy-start.1 = (f32[4,256,128]{2,1,0:T(8,128)S(1)}, f32[4,256,128]{2,1,0:T(8,128)}, u32[]{:S(2)}) copy-start(f32[4,256,128]{2,1,0:T(8,128)} %param.5) | copy-start | bytes 1572868
  167.8 6.9 %collective-permute-start = (f32[1,256,128]{2,1,0:T(8,128)S(1)}, f32[1,256,128]{2,1,0:T(8,128)S(1)}, u32[]{:S(2)}, u32[]{:S(2)}) collective-permute-start(f32[1,256,128]{2,1,0:T(8,128)S(1)} %slice.231), channel_id=1, source_target_pairs={{4,0},{8,4},{12,8},{5,1},{9,5},{13,9},{6,2},{10,6},{14,10},{7,3},{... | collective-permute-start | bytes 393224 | tf_op jit(solution)/shard_map/ppermute | solution.py:29
  175.0 4.0 %collective-permute-start.1 = (f32[1,256,128]{2,1,0:T(8,128)S(1)}, f32[1,256,128]{2,1,0:T(8,128)S(1)}, u32[]{:S(2)}, u32[]{:S(2)}) collective-permute-start(f32[1,256,128]{2,1,0:T(8,128)S(1)} %slice.232), channel_id=1, source_target_pairs={{0,4},{4,8},{8,12},{1,5},{5,9},{9,13},{2,6},{6,10},{10,14},{3,7},{... | collective-permute-start | bytes 393224 | tf_op jit(solution)/shard_map/ppermute | solution.py:29
  179.4 7.3 %collective-permute-start.2 = (f32[1,256,128]{2,1,0:T(8,128)S(1)}, f32[1,256,128]{2,1,0:T(8,128)S(1)}, u32[]{:S(2)}, u32[]{:S(2)}) collective-permute-start(f32[1,256,128]{2,1,0:T(8,128)S(1)} %slice.239), channel_id=1, source_target_pairs={{4,0},{8,4},{12,8},{5,1},{9,5},{13,9},{6,2},{10,6},{14,10},{7,3},{... | collective-permute-start | bytes 393224 | tf_op jit(solution)/shard_map/ppermute | solution.py:29
  187.1 6.4 %collective-permute-start.3 = (f32[1,256,128]{2,1,0:T(8,128)S(1)}, f32[1,256,128]{2,1,0:T(8,128)S(1)}, u32[]{:S(2)}, u32[]{:S(2)}) collective-permute-start(f32[1,256,128]{2,1,0:T(8,128)S(1)} %slice.240), channel_id=1, source_target_pairs={{0,4},{4,8},{8,12},{1,5},{5,9},{9,13},{2,6},{6,10},{10,14},{3,7},{... | collective-permute-start | bytes 393224 | tf_op jit(solution)/shard_map/ppermute | solution.py:29
  193.9 7.3 %collective-permute-start.4 = (f32[1,256,128]{2,1,0:T(8,128)S(1)}, f32[1,256,128]{2,1,0:T(8,128)S(1)}, u32[]{:S(2)}, u32[]{:S(2)}) collective-permute-start(f32[1,256,128]{2,1,0:T(8,128)S(1)} %slice.247), channel_id=1, source_target_pairs={{4,0},{8,4},{12,8},{5,1},{9,5},{13,9},{6,2},{10,6},{14,10},{7,3},{... | collective-permute-start | bytes 393224 | tf_op jit(solution)/shard_map/ppermute | solution.py:29
  201.6 6.4 %collective-permute-start.5 = (f32[1,256,128]{2,1,0:T(8,128)S(1)}, f32[1,256,128]{2,1,0:T(8,128)S(1)}, u32[]{:S(2)}, u32[]{:S(2)}) collective-permute-start(f32[1,256,128]{2,1,0:T(8,128)S(1)} %slice.248), channel_id=1, source_target_pairs={{0,4},{4,8},{8,12},{1,5},{5,9},{9,13},{2,6},{6,10},{10,14},{3,7},{... | collective-permute-start | bytes 393224 | tf_op jit(solution)/shard_map/ppermute | solution.py:29
  208.4 7.3 %collective-permute-start.6 = (f32[1,256,128]{2,1,0:T(8,128)S(1)}, f32[1,256,128]{2,1,0:T(8,128)S(1)}, u32[]{:S(2)}, u32[]{:S(2)}) collective-permute-start(f32[1,256,128]{2,1,0:T(8,128)S(1)} %slice.255), channel_id=1, source_target_pairs={{4,0},{8,4},{12,8},{5,1},{9,5},{13,9},{6,2},{10,6},{14,10},{7,3},{... | collective-permute-start | bytes 393224 | tf_op jit(solution)/shard_map/ppermute | solution.py:29
  216.1 6.9 %collective-permute-start.7 = (f32[1,256,128]{2,1,0:T(8,128)S(1)}, f32[1,256,128]{2,1,0:T(8,128)S(1)}, u32[]{:S(2)}, u32[]{:S(2)}) collective-permute-start(f32[1,256,128]{2,1,0:T(8,128)S(1)} %slice.256), channel_id=1, source_target_pairs={{0,4},{4,8},{8,12},{1,5},{5,9},{9,13},{2,6},{6,10},{10,14},{3,7},{... | collective-permute-start | bytes 393224 | tf_op jit(solution)/shard_map/ppermute | solution.py:29
  223.3 8.7 %collective-permute-start.8 = (f32[1,256,128]{2,1,0:T(8,128)S(1)}, f32[1,256,128]{2,1,0:T(8,128)S(1)}, u32[]{:S(2)}, u32[]{:S(2)}) collective-permute-start(f32[1,256,128]{2,1,0:T(8,128)S(1)} %slice.263), channel_id=1, source_target_pairs={{4,0},{8,4},{12,8},{5,1},{9,5},{13,9},{6,2},{10,6},{14,10},{7,3},{... | collective-permute-start | bytes 393224 | tf_op jit(solution)/shard_map/ppermute | solution.py:29
  232.4 6.6 %collective-permute-start.9 = (f32[1,256,128]{2,1,0:T(8,128)S(1)}, f32[1,256,128]{2,1,0:T(8,128)S(1)}, u32[]{:S(2)}, u32[]{:S(2)}) collective-permute-start(f32[1,256,128]{2,1,0:T(8,128)S(1)} %slice.264), channel_id=1, source_target_pairs={{0,4},{4,8},{8,12},{1,5},{5,9},{9,13},{2,6},{6,10},{10,14},{3,7},{... | collective-permute-start | bytes 393224 | tf_op jit(solution)/shard_map/ppermute | solution.py:29
  239.4 7.3 %collective-permute-start.10 = (f32[1,256,128]{2,1,0:T(8,128)S(1)}, f32[1,256,128]{2,1,0:T(8,128)S(1)}, u32[]{:S(2)}, u32[]{:S(2)}) collective-permute-start(f32[1,256,128]{2,1,0:T(8,128)S(1)} %slice.271), channel_id=1, source_target_pairs={{4,0},{8,4},{12,8},{5,1},{9,5},{13,9},{6,2},{10,6},{14,10},{7,3},{... | collective-permute-start | bytes 393224 | tf_op jit(solution)/shard_map/ppermute | solution.py:29
  247.1 6.4 %collective-permute-start.11 = (f32[1,256,128]{2,1,0:T(8,128)S(1)}, f32[1,256,128]{2,1,0:T(8,128)S(1)}, u32[]{:S(2)}, u32[]{:S(2)}) collective-permute-start(f32[1,256,128]{2,1,0:T(8,128)S(1)} %slice.272), channel_id=1, source_target_pairs={{0,4},{4,8},{8,12},{1,5},{5,9},{9,13},{2,6},{6,10},{10,14},{3,7},{... | collective-permute-start | bytes 393224 | tf_op jit(solution)/shard_map/ppermute | solution.py:29
Sparse Core Ops, SparseCore 0:
  119.6 32.1 all-reduce.26

commit v2 on v1

--- a/solution.py
+++ b/solution.py
@@ -78,10 +78,13 @@
     return field
 
 
-def two_pieces(value):
-    high = value.astype(jnp.bfloat16)
-    low = (value - high.astype(jnp.float32)).astype(jnp.bfloat16)
-    return high, low
+def three_pieces(value):
+    pieces = []
+    for _ in range(2):
+        piece = value.astype(jnp.bfloat16)
+        pieces.append(piece)
+        value = value - piece.astype(jnp.float32)
+    return pieces + [value.astype(jnp.bfloat16)]
 
 
 def one_hot_rows(cells, layers, rows, first_row, height, width):
@@ -136,10 +139,10 @@
 
 
 def inject(spread, values, injected):
-    high, low = two_pieces(values)
-    injected[...] = jnp.dot(spread[...], high, preferred_element_type=jnp.float32) + jnp.dot(
-        spread[...], low, preferred_element_type=jnp.float32
-    )
+    high, middle, low = [
+        jnp.dot(spread[...], piece, preferred_element_type=jnp.float32) for piece in three_pieces(values)
+    ]
+    injected[...] = high + (middle + low)
 
 
 def forward_kernel(
@@ -164,7 +167,7 @@
         values = field[2 : 2 + layers, halo : halo + own, :].reshape(cells, width)
         found = [
             jnp.dot(pick[...], piece, preferred_element_type=jnp.float32)
-            for piece in two_pieces(values)
+            for piece in three_pieces(values)
         ]
         pieces = [piece * mask for piece in found]
         total = jnp.zeros((8, column.shape[0]), jnp.float32)
@@ -221,6 +224,330 @@
     hot = (lane[:, None] == jnp.arange(width, dtype=jnp.int32)[None]).astype(jnp.float32)
     spread = [pairs[:, half, :, None] * hot[None] for half in range(2)]
     return jnp.concatenate(spread, axis=2)
+
+
+def peers_barrier(peers):
+    barrier = pltpu.get_barrier_semaphore()
+    for peer in peers:
+        pl.semaphore_signal(barrier, inc=1, device_id=peer, device_id_type=pl.DeviceIdType.MESH)
+    pl.semaphore_wait(barrier, len(peers))
+
+
+def remote(source, target, send, receive, peer):
+    return pltpu.make_async_remote_copy(
+        src_ref=source,
+        dst_ref=target,
+        send_sem=send,
+        recv_sem=receive,
+        device_id=peer,
+        device_id_type=pl.DeviceIdType.MESH,
+    )
+
+
+def model_kernel(subs, own, wide, model, send, receive, local):
+    me = lax.axis_index("sub")
+    slab = wide.shape[0]
+    rows = model.shape[1]
+    peers = [{"sub": lax.rem(me + d, subs)} for d in range(1, subs)]
+    peers_barrier(peers)
+    place = model.at[pl.ds(me * slab, slab)]
+
+    def rows_of(sub):
+        return wide.at[:, pl.ds(pl.multiple_of(sub * own, 8), rows), :]
+
+    copies = []
+    for d, peer in enumerate(peers):
+        copy = remote(rows_of(peer["sub"]), place, send.at[d], receive.at[d], peer)
+        copy.start()
+        copies.append(copy)
+    mine = pltpu.make_async_copy(rows_of(me), place, local)
+    mine.start()
+    mine.wait()
+    for d, copy in enumerate(copies):
+        copy.wait_send()
+        origin = lax.rem(me + subs - d - 1, subs)
+        remote(
+            rows_of(me), model.at[pl.ds(origin * slab, slab)], send.at[d], receive.at[d], peers[d]
+        ).wait_recv()
+
+
+def record_kernel(subs, record, observed, misfit, slots, send, receive):
+    me = lax.axis_index("sub")
+    peers = [{"sub": lax.rem(me + d, subs)} for d in range(1, subs)]
+    peers_barrier(peers)
+    copies = []
+    for d, peer in enumerate(peers):
+        copy = remote(record, slots.at[d], send.at[d], receive.at[d], peer)
+        copy.start()
+        copies.append(copy)
+    total = record[...]
+    for d, copy in enumerate(copies):
+        copy.wait()
+        total = total + slots[d]
+    misfit[...] = total - observed[...]
+
+
+def update_kernel(
+    geometry, subs, shots, part, model, updated, gradient,
+    near, own_model, strip, squares, arrived_squares, above, below,
+    field, extrap, target, dual_x, dual_y, dual_z, strip_out, slab_out, brick,
+    local, send_sum, get_sum, send_square, get_square, send_halo, get_halo,
+    send_brick, get_brick, send_slab, get_slab, send_on, get_on,
+):
+    layers, rows, own, halo, height, width = geometry
+    slab = layers // subs
+    lines = own // shots
+    sub, shot = lax.axis_index("sub"), lax.axis_index("shot")
+
+    def at(d_sub, d_shot):
+        return {"sub": lax.rem(sub + d_sub, subs), "shot": lax.rem(shot + d_shot, shots)}
+
+    def tiles(first):
+        return pl.ds(pl.multiple_of(first, 8), lines)
+
+    group = [(a, b) for a in range(subs) for b in range(shots) if (a, b) != (0, 0)]
+    fetch = pltpu.make_async_copy(
+        model.at[:, pl.ds(pl.multiple_of(halo + shot * lines - 8, 8), lines + 16), :], own_model, local
+    )
+    fetch.start()
+    peers_barrier([at(a, b) for a, b in group])
+
+    copies = []
+    for d in range(1, shots):
+        peer = at(0, d)
+        copy = remote(
+            part.at[:, tiles(peer["shot"] * lines), :], near.at[d - 1], send_sum.at[d - 1], get_sum.at[d - 1], peer
+        )
+        copy.start()
+        copies.append(copy)
+    for copy in copies:
+        copy.wait()
+    square = jnp.zeros((8, width), jnp.float32)
+    for layer in range(layers):
+        value = part[layer, tiles(shot * lines), :]
+        for d in range(shots - 1):
+            value = value + near[d, layer]
+        strip[layer] = value
+        for begin in range(0, lines, 8):
+            square = square + value[begin : begin + 8] * value[begin : begin + 8]
+    squares[...] = square
+
+    number = sub * shots + shot
+    count = subs * shots
+    halos = []
+    for way, (step, begin, place) in enumerate(((1, lines - 8, above), (count - 1, 0, below))):
+        other = lax.rem(number + step, count)
+        peer = {"sub": other // shots, "shot": lax.rem(other, shots)}
+        copy = remote(
+            strip.at[:, pl.ds(begin, 8), :], place, send_halo.at[way], get_halo.at[way], peer
+        )
+        copy.start()
+        halos.append(copy)
+    sums = []
+    for slot, (a, b) in enumerate(group):
+        copy = remote(squares, arrived_squares.at[slot], send_square.at[slot], get_square.at[slot], at(a, b))
+        copy.start()
+        sums.append(copy)
+    here = sub == shot
+    bricks = []
+    for d in range(subs):
+        peer = {"sub": lax.rem(sub + d, subs), "shot": sub}
+        bricks.append(
+            remote(
+                strip.at[pl.ds(peer["sub"] * slab, slab)],
+                brick.at[:, tiles(shot * lines), :],
+                send_brick.at[d],
+                get_brick.at[shot],
+                peer,
+            )
+        )
+    for copy in bricks[1:]:
+        copy.start()
+
+    @pl.when(jnp.logical_not(here))
+    def _():
+        bricks[0].start()
+
+    @pl.when(here)
+    def _():
+        brick[:, tiles(shot * lines), :] = strip[pl.ds(sub * slab, slab)]
+
+    for copy in sums + halos:
+        copy.wait()
+    total = squares[...]
+    for slot in range(len(group)):
+        total = total + arrived_squares[slot]
+    total = jnp.sum(total, axis=(0, 1), keepdims=True)
+    factor = step_length / jnp.sqrt(total / (layers * height * width) + epsilon)
+    fetch.wait()
+
+    tall = lines + 16
+    for layer in range(layers):
+        value = jnp.concatenate([above[layer], strip[layer], below[layer]], 0)
+        value = own_model[layer] - factor * value
+        target[layer] = value
+        value = jnp.clip(value, lower_bound, upper_bound)
+        field[layer] = value
+        extrap[layer] = value
+        for dual in (dual_x, dual_y, dual_z):
+            dual[layer] = jnp.zeros((tall, width), jnp.float32)
+    grid_row = lax.broadcasted_iota(jnp.int32, (tall, 1), 0) + (number * lines - 8)
+    row_weight = jnp.where(jnp.logical_and(grid_row >= 0, grid_row < height - 1), dual_step, 0.0)
+    lane = lax.broadcasted_iota(jnp.int32, (1, width), 1)
+    lane_weight = jnp.where(lane < width - 1, dual_step, 0.0)
+
+    def iteration(turn, carry):
+        before = jnp.zeros((tall, width), jnp.float32)
+        for layer in range(layers):
+            value = extrap[layer]
+            along_x = before
+            if layer < layers - 1:
+                along_x = dual_x[layer] + dual_step * (extrap[layer + 1] - value)
+                along_x = jnp.clip(along_x, -tv_bound, tv_bound)
+                dual_x[layer] = along_x
+            else:
+                along_x = jnp.zeros_like(before)
+            along_y = dual_y[layer] + row_weight * (pltpu.roll(value, tall - 1, 0) - value)
+            along_y = jnp.clip(along_y, -tv_bound, tv_bound)
+            dual_y[layer] = along_y
+            along_z = dual_z[layer] + lane_weight * (pltpu.roll(value, width - 1, 1) - value)
+            along_z = jnp.clip(along_z, -tv_bound, tv_bound)
+            dual_z[layer] = along_z
+            adjoint = (
+                (before - along_x)
+                + (pltpu.roll(along_y, 1, 0) - along_y)
+                + (pltpu.roll(along_z, 1, 1) - along_z)
+            )
+            old = field[layer]
+            new = (old - primal_step * adjoint + primal_step * target[layer]) * (1.0 / (1.0 + primal_step))
+            new = jnp.clip(new, lower_bound, upper_bound)
+            extrap[layer] = 2.0 * new - old
+            field[layer] = new
+            before = along_x
+        return carry
+
+    lax.fori_loop(0, ITERS, iteration, 0)
+    for layer in range(layers):
+        strip_out[layer] = field[layer, 8 : 8 + lines]
+
+    def place(d_sub, d_shot):
+        origin_sub = lax.rem(sub + subs - d_sub, subs)
+        origin_shot = lax.rem(shot + shots - d_shot, shots)
+        return slab_out.at[:, tiles(origin_sub * own + origin_shot * lines), :]
+
+    slabs = []
+    for d in range(1, subs):
+        peer = at(d, 0)
+        copy = remote(
+            strip_out.at[pl.ds(peer["sub"] * slab, slab)], place(0, 0), send_slab.at[d - 1], get_slab.at[d - 1], peer
+        )
+        copy.start()
+        slabs.append(copy)
+    slab_out[:, tiles(sub * own + shot * lines), :] = strip_out[pl.ds(sub * slab, slab)]
+    onward = []
+    for d in range(subs):
+        if d > 0:
+            remote(
+                strip_out.at[pl.ds(sub * slab, slab)], place(d, 0), send_slab.at[d - 1], get_slab.at[d - 1], at(d, 0)
+            ).wait_recv()
+        for e in range(1, shots):
+            copy = remote(place(d, 0), place(d, 0), send_on.at[d, e - 1], get_on.at[d, e - 1], at(0, e))
+            copy.start()
+            onward.append((d, e, copy))
+    for copy in bricks[1:]:
+        copy.wait_send()
+
+    @pl.when(jnp.logical_not(here))
+    def _():
+        bricks[0].wait_send()
+
+    for origin in range(shots):
+
+        @pl.when(jnp.logical_not(jnp.logical_and(here, shot == origin)))
+        def _():
+            remote(
+                strip.at[pl.ds(0, slab)],
+                brick.at[:, pl.ds(origin * lines, lines), :],
+                send_brick.at[0],
+                get_brick.at[origin],
+                at(1, 0),
+            ).wait_recv()
+
+    gradient[...] = brick[...]
+    for copy in slabs:
+        copy.wait_send()
+    for d, e, copy in onward:
+        copy.wait_send()
+        remote(place(d, e), place(d, e), send_on.at[d, e - 1], get_on.at[d, e - 1], at(0, e)).wait_recv()
+    updated[...] = slab_out[...]
+
+
+def update_by_strips(part, model, geometry, subs, shots, params):
+    layers, rows, own, halo, height, width = geometry
+    slab, lines = layers // subs, own // shots
+    tall = lines + 16
+    vmem = pl.BlockSpec(memory_space=pltpu.VMEM)
+
+    def space(*shape):
+        return pltpu.VMEM(shape, jnp.float32)
+
+    def sems(*shape):
+        return pltpu.SemaphoreType.DMA(shape)
+
+    others = subs * shots - 1
+    return pl.pallas_call(
+        functools.partial(update_kernel, geometry, subs, shots),
+        out_shape=(
+            jax.ShapeDtypeStruct((slab, height, width), jnp.float32),
+            jax.ShapeDtypeStruct((slab, own, width), jnp.float32),
+        ),
+        in_specs=[vmem, pl.BlockSpec(memory_space=pl.ANY)],
+        out_specs=(vmem, vmem),
+        scratch_shapes=[
+            space(shots - 1, layers, lines, width),
+            space(layers, tall, width),
+            space(layers, lines, width),
+            space(8, width),
+            space(others, 8, width),
+            space(layers, 8, width),
+            space(layers, 8, width),
+        ]
+        + [space(layers, tall, width)] * 6
+        + [space(layers, lines, width), space(slab, height, width), space(slab, own, width)]
+        + [pltpu.SemaphoreType.DMA]
+        + [sems(shots - 1)] * 2
+        + [sems(others)] * 2
+        + [sems(2)] * 2
+        + [sems(subs), sems(shots)]
+        + [sems(subs - 1)] * 2
+        + [sems(subs, shots - 1)] * 2,
+        compiler_params=params(2),
+    )(part, model)
+
+
+def update_by_slabs(part, model_field, geometry, subs):
+    layers, rows, own, halo, height, width = geometry
+    slab = layers // subs
+    local_gradient = lax.all_to_all(part.reshape(subs, slab, own, width), "sub", 0, 0)
+    local_gradient = jnp.swapaxes(local_gradient, 0, 1).reshape(slab, height, width)
+    last_x = lax.axis_index("sub") == subs - 1
+    slab_gradient = lax.psum(local_gradient, "shot")
+    square_sum = lax.psum(jnp.sum(slab_gradient * slab_gradient), "sub")
+    grad_scale = jnp.sqrt(square_sum / (layers * height * width) + epsilon)
+    target = model_field - step_length * (slab_gradient / grad_scale)
+
+    def slab_upper(layer):
+        return from_behind(layer, "sub", -1)
+
+    def slab_lower(layer):
+        return from_behind(layer, "sub", 1)
+
+    updated_model = project(target, slab_upper, slab_lower, last_x)
+    brick_rows = height // lax.axis_size("shot")
+    gradient = lax.dynamic_slice_in_dim(
+        slab_gradient, lax.axis_index("shot") * brick_rows, brick_rows, 1
+    )
+    return (updated_model, gradient)
 
 
 def per_device(model_field, source_index, wavelets, receiver_index, observed):
@@ -234,10 +561,21 @@
     geometry = (layers, rows, own, halo, height, width)
 
     wide = jnp.pad(model_field, ((0, 0), (halo, halo), (0, 0)))
-    parts = jnp.stack([wide[:, j * own : j * own + rows] for j in range(subs)])
-    model = lax.all_to_all(parts, "sub", 0, 0).reshape(layers, rows, width)
+    def remote_params(number):
+        return pltpu.CompilerParams(
+            collective_id=number, has_side_effects=True, vmem_limit_bytes=VMEM_LIMIT
+        )
 
     vmem = pl.BlockSpec(memory_space=pltpu.VMEM)
+    model = pl.pallas_call(
+        functools.partial(model_kernel, subs, own),
+        out_shape=jax.ShapeDtypeStruct((layers, rows, width), jnp.float32),
+        in_specs=[vmem],
+        out_specs=vmem,
+        scratch_shapes=[pltpu.SemaphoreType.DMA((subs - 1,))] * 2 + [pltpu.SemaphoreType.DMA],
+        compiler_params=remote_params(0),
+    )(wide)
+
     field = pltpu.VMEM((layers + 4, rows, width), jnp.float32)
     injected = pltpu.VMEM((layers * rows, 2 * width), jnp.float32)
     params = pltpu.CompilerParams(vmem_limit_bytes=VMEM_LIMIT)
@@ -260,7 +598,15 @@
         ],
         compiler_params=params,
     )(model, sources, receivers.reshape(-1, 1), values)
-    misfit = lax.psum(record, "sub") - observed[0]
+    misfit = pl.pallas_call(
+        functools.partial(record_kernel, subs),
+        out_shape=jax.ShapeDtypeStruct(record.shape, jnp.float32),
+        in_specs=[vmem, vmem],
+        out_specs=vmem,
+        scratch_shapes=[pltpu.VMEM((subs - 1,) + record.shape, jnp.float32)]
+        + [pltpu.SemaphoreType.DMA((subs - 1,))] * 2,
+        compiler_params=remote_params(1),
+    )(record, observed[0])
     values = spread_values(misfit[::-1], receivers[0], width)
     part_gradient = pl.pallas_call(
         functools.partial(backward_kernel, geometry),
@@ -276,26 +622,10 @@
         compiler_params=params,
     )(model, receivers, values, laps)
 
-    local_gradient = lax.all_to_all(part_gradient.reshape(subs, slab, own, width), "sub", 0, 0)
-    local_gradient = jnp.swapaxes(local_gradient, 0, 1).reshape(slab, height, width)
-    last_x = lax.axis_index("sub") == subs - 1
-    slab_gradient = lax.psum(local_gradient, "shot")
-    square_sum = lax.psum(jnp.sum(slab_gradient * slab_gradient), "sub")
-    grad_scale = jnp.sqrt(square_sum / (slab * height * width * subs) + epsilon)
-    target = model_field - step_length * (slab_gradient / grad_scale)
-
-    def slab_upper(layer):
-        return from_behind(layer, "sub", -1)
-
-    def slab_lower(layer):
-        return from_behind(layer, "sub", 1)
-
-    updated_model = project(target, slab_upper, slab_lower, last_x)
-    brick_rows = height // lax.axis_size("shot")
-    gradient = lax.dynamic_slice_in_dim(
-        slab_gradient, lax.axis_index("shot") * brick_rows, brick_rows, 1
-    )
-    return (updated_model, gradient)
+    shots = lax.axis_size("shot")
+    if subs == shots and own % (8 * shots) == 0:
+        return update_by_strips(part_gradient, model, geometry, subs, shots, remote_params)
+    return update_by_slabs(part_gradient, model_field, geometry, subs)
 
 
 def solution(mesh):

time: 262 us -> 136 us (0.52)
  waiting for transfers between devices: 101 us -> 0 us
  Pallas kernels: 44.3 us -> 118 us
  blocking collectives: 43.9 us -> 0 us
  starting transfers between devices: 35.2 us -> 0 us
  between operations: 15.3 us -> 0.74 us
  other arithmetic: 13.9 us -> 6.82 us
    pallas_call x0 -> x3, Pallas kernels: none -> 64.6 us  [the longest x1 30 us: update_by_strips(): pl.pallas_call(functools.partial(update_kernel, geometry, subs, shots), o...]
    ppermute x12 -> x0, waiting for transfers between devices: 49 us -> none  [from_behind(): lax.ppermute(value, axis, [(source, source + steps) for source in range(i...]
    psum x1 -> x0, waiting for transfers between devices: 32.3 us -> none  [per_device(): slab_gradient = lax.psum(local_gradient, 'shot')]
    psum x2 -> x0, blocking collectives: 30 us -> none  [the longest x1 17.7 us: per_device(): misfit = lax.psum(record, 'sub') - observed[0]]
    ppermute x12 -> x0, starting transfers between devices: 28.9 us -> none  [from_behind(): lax.ppermute(value, axis, [(source, source + steps) for source in range(i...]
    all_to_all x1 -> x0, waiting for transfers between devices: 20 us -> none  [per_device(): model = lax.all_to_all(parts, 'sub', 0, 0).reshape(layers, rows, width)]
    all_to_all x1 -> x0, blocking collectives: 13.9 us -> none  [per_device(): lax.all_to_all(part_gradient.reshape(subs, slab, own, width), 'sub', 0, 0)]
    pallas_call x1, Pallas kernels: 23.7 us -> 30.4 us  [per_device(): pl.pallas_call(functools.partial(forward_kernel, geometry), out_shape=(ja...]
  transfers between devices with their start and end apart: 14 -> 0, of which waited for: 14 -> 0; matrix products, arithmetic and copies ran while one was open for 2% -> 0% of each run, Pallas kernels for 0% -> 0%
where the time goes in v2:
time: 136 us; the launch traced here: 135 us
  Pallas kernels  118 us (87%)
  local copies, waits for them, and re-layouts  9.78 us (7%)
  other arithmetic  6.82 us (5%)
    pallas_call x1, Pallas kernels, per_device(): pl.pallas_call(functools.partial(forward_kernel, geometry), out_shape=(ja...  30.4 us
    pallas_call x1, Pallas kernels, update_by_strips(): pl.pallas_call(functools.partial(update_kernel, geometry, subs, shots), o...  30 us
    pallas_call x1, Pallas kernels, per_device(): pl.pallas_call(functools.partial(model_kernel, subs, own), out_shape=jax....  22.8 us
    pallas_call x1, Pallas kernels, per_device(): pl.pallas_call(functools.partial(backward_kernel, geometry), out_shape=ja...  22.6 us
    pallas_call x1, Pallas kernels, per_device(): pl.pallas_call(functools.partial(record_kernel, subs), out_shape=jax.Shap...  11.8 us
    unnamed x5, local copies, waits for them, and re-layouts  4.79 us
    concatenate x2, other arithmetic, spread_values(): return jnp.concatenate(spread, axis=2)  3.14 us

profile of v2, /device:TPU:0, one launch (start us, length us, event | category | flops | bytes accessed | tf_op | source)
XLA Modules:
  0.0 134.9 jit_solution(16999801703057224539)
XLA Ops:
  0.6 0.7 and_select_fusion
  1.3 0.7 add_select_fusion
  2.0 0.7 reduce
  2.8 1.4 %copy.27 = f32[1,12,512]{2,1,0:T(8,128)} copy(f32[1,12,512]{2,0,1:T(1,128)} %param.9) | data formatting | bytes 49152
  4.1 0.1 fusion.1
  4.3 0.1 fusion
  4.4 1.5 %copy.13.receivers_column = s32[512,1]{1,0:T(8,128)} copy(s32[512,1]{0,1:T(1,128)} %bitcast.20) | data formatting | bytes 4096 | tf_op jit(solution)/shard_map/reshape | solution.py:600
  5.9 1.9 %pad.4.wide = f32[4,304,128]{2,1,0:T(8,128)} pad(f32[4,256,128]{2,1,0:T(8,128)} %param.5, f32[]{:T(128)} %constant.22.clone.1), padding=0_0x24_24x0_0 | pad | bytes 1146884 | tf_op jit(solution)/shard_map/jit(_pad)/pad | solution.py:563
  7.8 22.8 %shard_map.68.model = f32[16,112,128]{2,1,0:T(8,128)} custom-call(f32[4,304,128]{2,1,0:T(8,128)} %pad.4.wide), custom_call_target="tpu_custom_call" | custom-call | tf_op jit(solution)/shard_map/pallas_call | solution.py:570
  30.7 0.5 broadcast_multiply_fusion.3
  31.2 1.2 pad_maximum_fusion.1.values
  32.4 30.4 %shard_map.69 = (f32[12,16,64,128]{3,2,1,0:T(8,128)}, f32[12,512]{1,0:T(8,128)}) custom-call(f32[16,112,128]{2,1,0:T(8,128)} %shard_map.68.model, s32[1,256]{1,0:T(1,128)} %sources.1, s32[512,1]{1,0:T(8,128)} %copy.13.receivers_column, f32[6,256,256]{2,1,0:T(8,128)} %pad_maximum_fusion.1.values), custom_call_target="tpu_custom_call" | custom-call | tf_op jit(solution)/shard_map/pallas_call | solution.py:584
  62.8 11.8 %shard_map.70 = f32[12,512]{1,0:T(8,128)} custom-call(f32[12,512]{1,0:T(8,128)} %get-tuple-element.4.record, f32[12,512]{1,0:T(8,128)} %bitcast.16), custom_call_target="tpu_custom_call" | custom-call | tf_op jit(solution)/shard_map/pallas_call | solution.py:601
  74.6 1.5 %rev.3 = f32[12,512]{1,0:T(8,128)S(1)} reverse(f32[12,512]{1,0:T(8,128)} %shard_map.70), dimensions={0} | reverse | bytes 49152 | tf_op jit(solution)/shard_map/rev | solution.py:610
  76.2 0.9 broadcast_multiply_fusion.1
  77.0 1.9 %pad_maximum_fusion.values = f32[6,512,256]{2,1,0:T(8,128)} fusion(f32[6,512,128]{2,1,0:T(8,128)S(1)} %get-tuple-element.7, f32[6,512,128]{2,1,0:T(8,128)S(1)} %get-tuple-element.6), kind=kLoop, calls=%fused_computation | loop fusion | flops 786432 | bytes 6291456 | tf_op jit(solution)/shard_map/concatenate | solution.py:226
  78.9 22.6 %shard_map.71.part = f32[16,64,128]{2,1,0:T(8,128)} custom-call(f32[16,112,128]{2,1,0:T(8,128)} %shard_map.68.model, s32[1,512]{1,0:T(1,128)} %receivers.1, f32[6,512,256]{2,1,0:T(8,128)} %pad_maximum_fusion.values, f32[12,16,64,128]{3,2,1,0:T(8,128)} %get-tuple-element.5.laps), custom_call_target="tpu_custom_call" | custom-call | tf_op jit(solution)/shard_map/pallas_call | solution.py:611
  101.5 30.0 %shard_map.72 = (f32[4,256,128]{2,1,0:T(8,128)}, f32[4,64,128]{2,1,0:T(8,128)}) custom-call(f32[16,64,128]{2,1,0:T(8,128)} %shard_map.71.part, f32[16,112,128]{2,1,0:T(8,128)} %shard_map.68.model), custom_call_target="tpu_custom_call" | custom-call | tf_op jit(solution)/shard_map/pallas_call | solution.py:498
  131.5 1.9 %copy.32 = f32[4,256,128]{2,1,0:T(8,128)} copy(f32[4,256,128]{2,1,0:T(8,128)} %get-tuple-element.18) | data formatting | bytes 1048576
  133.4 1.6 %copy.33 = f32[4,64,128]{2,1,0:T(8,128)} copy(f32[4,64,128]{2,1,0:T(8,128)} %get-tuple-element.19) | data formatting | bytes 262144
  (7 shorter events, 0.1 us)

commit v3 on v2

v3 whole, which is shorter than its diff:
```python
import functools

import jax
import jax.numpy as jnp
from jax import lax
from jax.experimental import pallas as pl
from jax.experimental.pallas import tpu as pltpu
from jax.sharding import PartitionSpec as P

ITERS = 6

near_weight = 4.0 / 3.0
far_weight = -1.0 / 12.0
centre_weight = 7.5
step_length = 0.02
tv_bound = 0.01
dual_step = 0.25
primal_step = 0.25
lower_bound = 0.08
upper_bound = 0.22
epsilon = 1e-06

VMEM_LIMIT = 58 * 1024 * 1024


def from_behind(value, axis, steps):
    count = lax.axis_size(axis)
    initial, last = (max(0, -steps), min(count, count - steps))
    return lax.ppermute(value, axis, [(source, source + steps) for source in range(initial, last)])


def forward_part(field, along, upper, last_owner):
    size = field.shape[along]
    first_row = lax.slice_in_dim(field, 0, 1, axis=along)
    remainder = lax.slice_in_dim(field, 1, size, axis=along)
    beyond = jnp.zeros_like(first_row) if upper is None else upper(first_row)
    difference = jnp.concatenate([remainder, beyond], along) - field
    row_index = lax.broadcasted_iota(jnp.int32, field.shape, along)
    return jnp.where(jnp.logical_and(row_index == size - 1, last_owner), 0.0, difference)


def backward_part(dual, along, lower):
    size = dual.shape[along]
    last_row = lax.slice_in_dim(dual, size - 1, size, axis=along)
    before = jnp.zeros_like(last_row) if lower is None else lower(last_row)
    earlier = jnp.concatenate([before, lax.slice_in_dim(dual, 0, size - 1, axis=along)], along)
    return earlier - dual


def project(target, upper_x, lower_x, last_x):
    field = jnp.clip(target, lower_bound, upper_bound)
    extrap = field
    duals = [jnp.zeros_like(field) for along in range(3)]
    for iteration in range(ITERS):
        duals = [
            jnp.clip(
                duals[0] + dual_step * forward_part(extrap, 0, upper_x, last_x), -tv_bound, tv_bound
            ),
            jnp.clip(
                duals[1] + dual_step * forward_part(extrap, 1, None, True), -tv_bound, tv_bound
            ),
            jnp.clip(
                duals[2] + dual_step * forward_part(extrap, 2, None, True), -tv_bound, tv_bound
            ),
        ]
        adjoint = (
            backward_part(duals[0], 0, lower_x)
            + backward_part(duals[1], 1, None)
            + backward_part(duals[2], 2, None)
        )
        following = jnp.clip(
            (field - primal_step * adjoint + primal_step * target) / (1.0 + primal_step),
            lower_bound,
            upper_bound,
        )
        extrap = 2.0 * following - field
        field = following
    return field


def three_pieces(value):
    pieces = []
    for _ in range(2):
        piece = value.astype(jnp.bfloat16)
        pieces.append(piece)
        value = value - piece.astype(jnp.float32)
    return pieces + [value.astype(jnp.bfloat16)]


def one_hot_rows(cells, layers, rows, first_row, height, width):
    lines = cells // width
    layer = lines // height
    row = lines - layer * height - first_row
    inside = jnp.logical_and(row >= 0, row < rows)
    return jnp.where(inside, layer * rows + row, -1)


def advance(model, current, earlier, injected, column, extent, margin, keep, accumulate):
    layers, rows, own, width = extent
    low = (rows - own) // 2 - margin
    count = own + 2 * margin
    span = pl.ds(low, count)
    lane = lax.broadcasted_iota(jnp.int32, (1, width), 1)
    weights = [
        (1, jnp.where(lane >= 1, near_weight, 0.0)),
        (width - 1, jnp.where(lane < width - 1, near_weight, 0.0)),
        (2, jnp.where(lane >= 2, far_weight, 0.0)),
        (width - 2, jnp.where(lane < width - 2, far_weight, 0.0)),
    ]

    def layer_step(layer):
        centre = current[layer + 2, span]
        near = current[layer + 1, span] + current[layer + 3, span]
        far = current[layer, span] + current[layer + 4, span]
        near = near + (pltpu.roll(centre, 1, 0) + pltpu.roll(centre, count - 1, 0))
        far = far + (pltpu.roll(centre, 2, 0) + pltpu.roll(centre, count - 2, 0))
        lap = near_weight * near + far_weight * far - centre_weight * centre
        for shift, weight in weights:
            lap = lap + weight * pltpu.roll(centre, shift, 1)
        start = pl.multiple_of(layer * rows + low, 8)
        following = 2.0 * centre - earlier[layer + 2, span] + model[layer, span] * lap
        following = following + injected[pl.ds(start, count), pl.ds(column, width)]
        earlier[layer + 2, span] = following
        if keep is not None:
            keep(layer, lap[margin : margin + own])
        if accumulate is not None:
            accumulate(layer, following[margin : margin + own])

    block = 4

    def block_step(number, carry):
        for part in range(block):
            layer_step(number * block + part)
        return carry

    lax.fori_loop(0, layers // block, block_step, 0)


def fill_one_hot(target, positions):
    step = 256
    shape = (step, target.shape[1])

    def fill(number, carry):
        begin = pl.multiple_of(number * step, step)
        grid_row = lax.broadcasted_iota(jnp.int32, shape, 0) + begin
        target[pl.ds(begin, step), :] = jnp.where(grid_row == positions, 1.0, 0.0).astype(jnp.bfloat16)
        return carry

    lax.fori_loop(0, target.shape[0] // step, fill, 0)


def inject(spread, values, injected):
    pieces = three_pieces(values)
    blocks = max(1, spread.shape[0] // 896)
    size = spread.shape[0] // blocks

    def block(number, carry):
        span = pl.ds(pl.multiple_of(number * size, 16), size)
        high, middle, low = [
            jnp.dot(spread[span, :], piece, preferred_element_type=jnp.float32) for piece in pieces
        ]
        injected[span, :] = high + (middle + low)
        return carry

    lax.fori_loop(0, blocks, block, 0)


def pair_groups(steps, halo):
    margins = [min(halo, -(-2 * (steps - 1 - 2 * pair) // 8) * 8) for pair in range(steps // 2)]
    groups = []
    for pair, margin in enumerate(margins):
        if pair > 1 and groups[-1][2] == margin:
            groups[-1][1] = pair + 1
        else:
            groups.append([pair, pair + 1, margin])
    return groups


def propagate(
    geometry, subs, shots, model_field, sources, wavelets, receivers, observed,
    wide, model, laps, part, first, second, injected, source_spread, receiver_spread, pick,
    source_table, receiver_table, misfit_table, record, slots,
    send_model, get_model, send_swap, get_swap, send_record, get_record,
):
    layers, rows, own, halo, height, width = geometry
    sub, shot = lax.axis_index("sub"), lax.axis_index("shot")
    slab = layers // subs
    steps = wavelets.shape[0]
    half = slab // 2
    side = lax.rem(shot, 2)
    start_row = sub * own

    wide[:, :halo, :] = jnp.zeros((slab, halo, width), jnp.float32)
    wide[:, halo + height :, :] = jnp.zeros((slab, halo, width), jnp.float32)
    wide[:, halo : halo + height, :] = model_field[...]
    partner = {"sub": sub, "shot": shot + 1 - 2 * side}
    peers = [{"sub": lax.rem(sub + d, subs), "shot": shot} for d in range(1, subs)]

    def rows_of(other):
        return pl.ds(pl.multiple_of(other * own, 8), rows)

    def place(d, which):
        return model.at[pl.ds(lax.rem(sub + subs - d, subs) * slab + which * half, half)]

    sends = []
    for d, peer in enumerate(peers):
        copy = remote(
            wide.at[pl.ds(side * half, half), rows_of(peer["sub"]), :],
            place(0, side), send_model.at[d], get_model.at[d], peer,
        )
        copy.start()
        sends.append(copy)
    for layer in range(slab):
        model[sub * slab + layer] = wide[layer, rows_of(sub), :]

    first[...] = jnp.zeros_like(first)
    second[...] = jnp.zeros_like(second)
    part[...] = jnp.zeros_like(part)
    fill_one_hot(source_spread, one_hot_rows(sources[...], layers, rows, start_row - halo, height, width))

    def lanes_of(cells):
        return (cells - (cells // width) * width).astype(jnp.float32)

    source_table[...] = jnp.zeros_like(source_table)
    source_table[0:steps, :] = wavelets[...]
    source_table[pl.ds(steps, 1), :] = lanes_of(sources[...])
    source_columns = source_table[...].T
    receiver_table[...] = jnp.zeros_like(receiver_table)
    receiver_table[0:1, :] = lanes_of(receivers[...])
    receiver_table[1:2, :] = one_hot_rows(receivers[...], layers, own, start_row, height, width).astype(jnp.float32)
    receiver_columns = receiver_table[...].T
    source_lane = lax.broadcasted_iota(jnp.int32, source_columns.shape, 1)
    source_hot = jnp.where(source_lane.astype(jnp.float32) == source_columns[:, steps : steps + 1], 1.0, 0.0)
    receiver_lane = lax.broadcasted_iota(jnp.int32, receiver_columns.shape, 1)
    receiver_hot = jnp.where(receiver_lane.astype(jnp.float32) == receiver_columns[:, 0:1], 1.0, 0.0)
    cells = layers * own
    owned = receiver_columns[:, 1:2]
    for begin in range(0, cells, 256):
        numbers = lax.broadcasted_iota(jnp.int32, (owned.shape[0], 256), 1) + begin
        pick[:, begin : begin + 256] = jnp.where(numbers.astype(jnp.float32) == owned, 1.0, 0.0).astype(jnp.bfloat16)

    swaps = []
    for d in range(1, subs):
        remote(
            wide.at[pl.ds(side * half, half), rows_of(sub), :],
            place(d, side), send_model.at[d - 1], get_model.at[d - 1], peers[d - 1],
        ).wait_recv()
        copy = remote(place(d, side), place(d, side), send_swap.at[d - 1], get_swap.at[d - 1], partner)
        copy.start()
        swaps.append(copy)
    fill_one_hot(receiver_spread, one_hot_rows(receivers[...], layers, rows, start_row - halo, height, width))

    def column_values(columns, lanes, hot, step):
        return jnp.sum(jnp.where(lanes == step, columns, 0.0), axis=1, keepdims=True) * hot

    def initial(keep_laps):
        def fill(layer, carry):
            first[layer + 2] = injected[pl.ds(pl.multiple_of(layer * rows, 8), rows), pl.ds(0, width)]
            if keep_laps:
                laps[0, layer] = jnp.zeros((own, width), jnp.float32)
            else:
                accumulate(0)(layer, first[layer + 2, halo : halo + own])
            return carry

        lax.fori_loop(0, layers, fill, 0)

    def keep(step):
        def store(layer, lap):
            laps[step, layer] = lap

        return store

    def accumulate(step):
        def add(layer, following):
            part[layer] += following * laps[steps - 1 - step, layer]

        return add

    ones = jnp.ones((8, width), jnp.bfloat16)

    def sample(pair):
        values = [
            three_pieces(field[2 : 2 + layers, halo : halo + own, :].reshape(cells, width))
            for field in (first, second)
        ]
        totals = [jnp.zeros((8, owned.shape[0]), jnp.float32) for _ in range(2)]
        for pieces in zip(*values):
            found = jnp.dot(pick[...], jnp.concatenate(pieces, axis=1), preferred_element_type=jnp.float32)
            for which in range(2):
                piece = (found[:, which * width : (which + 1) * width] * receiver_hot).astype(jnp.bfloat16)
                totals[which] = totals[which] + lax.dot_general(
                    ones, piece, (((1,), (1,)), ((), ())), preferred_element_type=jnp.float32
                )
        for which in range(2):
            record[pl.ds(2 * pair + which, 1), :] = totals[which][0:1]

    extent = (layers, rows, own, width)
    arrived = []

    def run(forward, value_at, spread):
        for begin, end, margin in pair_groups(steps, halo):

            def pair_step(pair, carry):
                inject(spread, jnp.concatenate([value_at(2 * pair), value_at(2 * pair + 1)], axis=1), injected)
                for which, (current, earlier) in enumerate(((second, first), (first, second))):
                    step = 2 * pair + which
                    if begin == 0 and which == 0:
                        initial(forward)
                        if not arrived:
                            for d in range(1, subs):
                                remote(
                                    place(d, 1 - side), place(d, 1 - side),
                                    send_swap.at[d - 1], get_swap.at[d - 1], partner,
                                ).wait_recv()
                            arrived.append(True)
                        continue
                    advance(
                        model, current, earlier, injected, which * width, extent, margin,
                        keep(step) if forward else None, None if forward else accumulate(step),
                    )
                if forward:
                    sample(pair)
                return carry

            if begin == 0:
                pair_step(0, 0)
            else:
                lax.fori_loop(begin, end, pair_step, 0)

    run(True, lambda step: column_values(source_columns, source_lane, source_hot, step), source_spread)
    for copy in sends + swaps:
        copy.wait_send()

    copies = []
    for d, peer in enumerate(peers):
        copy = remote(record, slots.at[d], send_record.at[d], get_record.at[d], peer)
        copy.start()
        copies.append(copy)
    first[...] = jnp.zeros_like(first)
    second[...] = jnp.zeros_like(second)
    misfit_table[...] = jnp.zeros_like(misfit_table)
    total = record[...]
    for d, copy in enumerate(copies):
        copy.wait()
        total = total + slots[d]
    misfit_table[0:steps, :] = total - observed[...]
    misfit_columns = misfit_table[...].T
    run(
        False,
        lambda step: column_values(misfit_columns, receiver_lane, receiver_hot, steps - 1 - step),
        receiver_spread,
    )


def peers_barrier(peers):
    barrier = pltpu.get_barrier_semaphore()
    for peer in peers:
        pl.semaphore_signal(barrier, inc=1, device_id=peer, device_id_type=pl.DeviceIdType.MESH)
    pl.semaphore_wait(barrier, len(peers))


def remote(source, target, send, receive, peer):
    return pltpu.make_async_remote_copy(
        src_ref=source,
        dst_ref=target,
        send_sem=send,
        recv_sem=receive,
        device_id=peer,
        device_id_type=pl.DeviceIdType.MESH,
    )


def update(
    geometry, subs, shots, part, model, updated, gradient,
    near, strip, squares, arrived_squares, above, below,
    field, extrap, target, dual_x, dual_y, dual_z, strip_out, slab_out, brick,
    send_sum, get_sum, send_square, get_square, send_halo, get_halo,
    send_brick, get_brick, send_slab, get_slab, send_on, get_on,
):
    layers, rows, own, halo, height, width = geometry
    slab = layers // subs
    lines = own // shots
    sub, shot = lax.axis_index("sub"), lax.axis_index("shot")

    def at(d_sub, d_shot):
        return {"sub": lax.rem(sub + d_sub, subs), "shot": lax.rem(shot + d_shot, shots)}

    def tiles(first):
        return pl.ds(pl.multiple_of(first, 8), lines)

    group = [(a, b) for a in range(subs) for b in range(shots) if (a, b) != (0, 0)]
    copies = []
    for d in range(1, shots):
        peer = at(0, d)
        copy = remote(
            part.at[:, tiles(peer["shot"] * lines), :], near.at[d - 1], send_sum.at[d - 1], get_sum.at[d - 1], peer
        )
        copy.start()
        copies.append(copy)
    for copy in copies:
        copy.wait()
    square = jnp.zeros((8, width), jnp.float32)
    for layer in range(layers):
        value = part[layer, tiles(shot * lines), :]
        for d in range(shots - 1):
            value = value + near[d, layer]
        strip[layer] = value
        for begin in range(0, lines, 8):
            square = square + value[begin : begin + 8] * value[begin : begin + 8]
    squares[...] = square

    number = sub * shots + shot
    count = subs * shots
    halos = []
    for way, (step, begin, place) in enumerate(((1, lines - 8, above), (count - 1, 0, below))):
        other = lax.rem(number + step, count)
        peer = {"sub": other // shots, "shot": lax.rem(other, shots)}
        copy = remote(
            strip.at[:, pl.ds(begin, 8), :], place, send_halo.at[way], get_halo.at[way], peer
        )
        copy.start()
        halos.append(copy)
    sums = []
    for slot, (a, b) in enumerate(group):
        copy = remote(squares, arrived_squares.at[slot], send_square.at[slot], get_square.at[slot], at(a, b))
        copy.start()
        sums.append(copy)
    here = sub == shot
    bricks = []
    for d in range(subs):
        peer = {"sub": lax.rem(sub + d, subs), "shot": sub}
        bricks.append(
            remote(
                strip.at[pl.ds(peer["sub"] * slab, slab)],
                brick.at[:, tiles(shot * lines), :],
                send_brick.at[d],
                get_brick.at[shot],
                peer,
            )
        )
    for copy in bricks[1:]:
        copy.start()

    @pl.when(jnp.logical_not(here))
    def _():
        bricks[0].start()

    @pl.when(here)
    def _():
        brick[:, tiles(shot * lines), :] = strip[pl.ds(sub * slab, slab)]

    for copy in sums + halos:
        copy.wait()
    total = squares[...]
    for slot in range(len(group)):
        total = total + arrived_squares[slot]
    total = jnp.sum(total, axis=(0, 1), keepdims=True)
    factor = step_length / jnp.sqrt(total / (layers * height * width) + epsilon)
    beside = pl.ds(pl.multiple_of(halo + shot * lines - 8, 8), lines + 16)

    tall = lines + 16
    for layer in range(layers):
        value = jnp.concatenate([above[layer], strip[layer], below[layer]], 0)
        value = model[layer, beside] - factor * value
        target[layer] = value
        value = jnp.clip(value, lower_bound, upper_bound)
        field[layer] = value
        extrap[layer] = value
        for dual in (dual_x, dual_y, dual_z):
            dual[layer] = jnp.zeros((tall, width), jnp.float32)
    grid_row = lax.broadcasted_iota(jnp.int32, (tall, 1), 0) + (number * lines - 8)
    row_weight = jnp.where(jnp.logical_and(grid_row >= 0, grid_row < height - 1), dual_step, 0.0)
    lane = lax.broadcasted_iota(jnp.int32, (1, width), 1)
    lane_weight = jnp.where(lane < width - 1, dual_step, 0.0)

    def iteration(turn, carry):
        before = jnp.zeros((tall, width), jnp.float32)
        for layer in range(layers):
            value = extrap[layer]
            along_x = before
            if layer < layers - 1:
                along_x = dual_x[layer] + dual_step * (extrap[layer + 1] - value)
                along_x = jnp.clip(along_x, -tv_bound, tv_bound)
                dual_x[layer] = along_x
            else:
                along_x = jnp.zeros_like(before)
            along_y = dual_y[layer] + row_weight * (pltpu.roll(value, tall - 1, 0) - value)
            along_y = jnp.clip(along_y, -tv_bound, tv_bound)
            dual_y[layer] = along_y
            along_z = dual_z[layer] + lane_weight * (pltpu.roll(value, width - 1, 1) - value)
            along_z = jnp.clip(along_z, -tv_bound, tv_bound)
            dual_z[layer] = along_z
            adjoint = (
                (before - along_x)
                + (pltpu.roll(along_y, 1, 0) - along_y)
                + (pltpu.roll(along_z, 1, 1) - along_z)
            )
            old = field[layer]
            new = (old - primal_step * adjoint + primal_step * target[layer]) * (1.0 / (1.0 + primal_step))
            new = jnp.clip(new, lower_bound, upper_bound)
            extrap[layer] = 2.0 * new - old
            field[layer] = new
            before = along_x
        return carry

    lax.fori_loop(0, ITERS, iteration, 0)
    for layer in range(layers):
        strip_out[layer] = field[layer, 8 : 8 + lines]

    def place(d_sub, d_shot):
        origin_sub = lax.rem(sub + subs - d_sub, subs)
        origin_shot = lax.rem(shot + shots - d_shot, shots)
        return slab_out.at[:, tiles(origin_sub * own + origin_shot * lines), :]

    slabs = []
    for d in range(1, subs):
        peer = at(d, 0)
        copy = remote(
            strip_out.at[pl.ds(peer["sub"] * slab, slab)], place(0, 0), send_slab.at[d - 1], get_slab.at[d - 1], peer
        )
        copy.start()
        slabs.append(copy)
    slab_out[:, tiles(sub * own + shot * lines), :] = strip_out[pl.ds(sub * slab, slab)]
    onward = []
    for d in range(subs):
        if d > 0:
            remote(
                strip_out.at[pl.ds(sub * slab, slab)], place(d, 0), send_slab.at[d - 1], get_slab.at[d - 1], at(d, 0)
            ).wait_recv()
        for e in range(1, shots):
            copy = remote(place(d, 0), place(d, 0), send_on.at[d, e - 1], get_on.at[d, e - 1], at(0, e))
            copy.start()
            onward.append((d, e, copy))
    for copy in bricks[1:]:
        copy.wait_send()

    @pl.when(jnp.logical_not(here))
    def _():
        bricks[0].wait_send()

    for origin in range(shots):

        @pl.when(jnp.logical_not(jnp.logical_and(here, shot == origin)))
        def _():
            remote(
                strip.at[pl.ds(0, slab)],
                brick.at[:, pl.ds(origin * lines, lines), :],
                send_brick.at[0],
                get_brick.at[origin],
                at(1, 0),
            ).wait_recv()

    gradient[...] = brick[...]
    for copy in slabs:
        copy.wait_send()
    for d, e, copy in onward:
        copy.wait_send()
        remote(place(d, e), place(d, e), send_on.at[d, e - 1], get_on.at[d, e - 1], at(0, e)).wait_recv()
    updated[...] = slab_out[...]


PROPAGATE_SCRATCH = 21


def step_kernel(geometry, subs, shots, strips, *refs):
    inputs, refs = refs[:5], refs[5:]
    if strips:
        updated, gradient = refs[:2]
        scratch = refs[2:]
        laps_on = scratch[:3]
        part, scratch = scratch[3], scratch[4:]
    else:
        part, laps_on, scratch = refs[0], refs[1:4], refs[4:]
    wide, model, laps = laps_on
    own_scratch, rest = scratch[: PROPAGATE_SCRATCH - 4], scratch[PROPAGATE_SCRATCH - 4 :]
    sub, shot = lax.axis_index("sub"), lax.axis_index("shot")
    if strips:
        group = [(a, b) for a in range(subs) for b in range(shots) if (a, b) != (0, 0)]
        peers_barrier(
            [{"sub": lax.rem(sub + a, subs), "shot": lax.rem(shot + b, shots)} for a, b in group]
        )
    else:
        peers_barrier(
            [{"sub": lax.rem(sub + a, subs), "shot": shot} for a in range(1, subs)]
            + [{"sub": sub, "shot": shot + 1 - 2 * lax.rem(shot, 2)}]
        )
    propagate(geometry, subs, shots, *inputs, wide, model, laps, part, *own_scratch)
    if strips:
        update(geometry, subs, shots, part, model, updated, gradient, *rest)


def update_by_slabs(part, model_field, geometry, subs):
    layers, rows, own, halo, height, width = geometry
    slab = layers // subs
    local_gradient = lax.all_to_all(part.reshape(subs, slab, own, width), "sub", 0, 0)
    local_gradient = jnp.swapaxes(local_gradient, 0, 1).reshape(slab, height, width)
    last_x = lax.axis_index("sub") == subs - 1
    slab_gradient = lax.psum(local_gradient, "shot")
    square_sum = lax.psum(jnp.sum(slab_gradient * slab_gradient), "sub")
    grad_scale = jnp.sqrt(square_sum / (layers * height * width) + epsilon)
    target = model_field - step_length * (slab_gradient / grad_scale)

    def slab_upper(layer):
        return from_behind(layer, "sub", -1)

    def slab_lower(layer):
        return from_behind(layer, "sub", 1)

    updated_model = project(target, slab_upper, slab_lower, last_x)
    brick_rows = height // lax.axis_size("shot")
    gradient = lax.dynamic_slice_in_dim(
        slab_gradient, lax.axis_index("shot") * brick_rows, brick_rows, 1
    )
    return (updated_model, gradient)


def per_device(model_field, source_index, wavelets, receiver_index, observed):
    slab, height, width = model_field.shape
    subs, shots = lax.axis_size("sub"), lax.axis_size("shot")
    layers = slab * subs
    own = height // subs
    steps = wavelets.shape[1]
    halo = 2 * steps
    rows = own + 2 * halo
    geometry = (layers, rows, own, halo, height, width)
    points, receivers = source_index.shape[1], receiver_index.shape[1]
    strips = subs == shots and own % (8 * shots) == 0
    lines = own // shots
    tall = lines + 16
    others = subs * shots - 1
    vmem = pl.BlockSpec(memory_space=pltpu.VMEM)

    def space(*shape, dtype=jnp.float32):
        return pltpu.VMEM(shape, dtype)

    def sems(*shape):
        return pltpu.SemaphoreType.DMA(shape)

    scratch = [space(slab, height + 2 * halo, width), space(layers, rows, width), space(steps, layers, own, width)]
    if strips:
        scratch.append(space(layers, own, width))
    scratch += [
        space(layers + 4, rows, width),
        space(layers + 4, rows, width),
        space(layers * rows, 2 * width),
        space(layers * rows, points, dtype=jnp.bfloat16),
        space(layers * rows, receivers, dtype=jnp.bfloat16),
        space(receivers, layers * own, dtype=jnp.bfloat16),
        space(width, points),
        space(width, receivers),
        space(width, receivers),
        space(steps, receivers),
        space(subs - 1, steps, receivers),
    ] + [sems(subs - 1)] * 6
    if strips:
        scratch += [
            space(shots - 1, layers, lines, width),
            space(layers, lines, width),
            space(8, width),
            space(others, 8, width),
            space(layers, 8, width),
            space(layers, 8, width),
        ]
        scratch += [space(layers, tall, width)] * 6
        scratch += [space(layers, lines, width), space(slab, height, width), space(slab, own, width)]
        scratch += [sems(shots - 1)] * 2 + [sems(others)] * 2 + [sems(2)] * 2 + [sems(subs), sems(shots)]
        scratch += [sems(subs - 1)] * 2 + [sems(subs, shots - 1)] * 2
        out_shape = (
            jax.ShapeDtypeStruct((slab, height, width), jnp.float32),
            jax.ShapeDtypeStruct((slab, own, width), jnp.float32),
        )
        out_specs = (vmem, vmem)
    else:
        out_shape = jax.ShapeDtypeStruct((layers, own, width), jnp.float32)
        out_specs = vmem
    result = pl.pallas_call(
        functools.partial(step_kernel, geometry, subs, shots, strips),
        out_shape=out_shape,
        in_specs=[vmem] * 5,
        out_specs=out_specs,
        scratch_shapes=scratch,
        compiler_params=pltpu.CompilerParams(
            collective_id=0, has_side_effects=True, vmem_limit_bytes=VMEM_LIMIT
        ),
    )(model_field, source_index, wavelets[0], receiver_index, observed[0])
    if strips:
        return result
    return update_by_slabs(result, model_field, geometry, subs)


def solution(mesh):
    placed = (
        P(("grp", "sub"), None, None),
        P(("grp", "shot"), None),
        P(("grp", "shot"), None, None),
        P(("grp", "shot"), None),
        P(("grp", "shot"), None, None),
    )
    return jax.shard_map(
        per_device,
        mesh=mesh,
        in_specs=placed,
        out_specs=(P(("grp", "sub"), None, None), P(("grp", "sub"), "shot", None)),
        check_vma=False,
    )
```

time: 136 us -> 108 us (0.79)
  Pallas kernels: 118 us -> 103 us
  other arithmetic: 6.82 us -> 0 us
  local copies, waits for them, and re-layouts: 9.78 us -> 4.5 us
    pallas_call x5 -> x1, Pallas kernels: 118 us -> 103 us  [per_device(): pl.pallas_call(functools.partial(step_kernel, geometry, subs, shots, stri...]
    concatenate x2 -> x0, other arithmetic: 3.14 us -> none  [spread_values(): return jnp.concatenate(spread, axis=2)]
    pad x1 -> x0, local copies, waits for them, and re-layouts: 1.92 us -> none  [per_device(): wide = jnp.pad(model_field, ((0, 0), (halo, halo), (0, 0)))]
    reshape x2 -> x0, local copies, waits for them, and re-layouts: 1.56 us -> none  [the longest x1 1.54 us: per_device(): receivers.reshape(-1, 1)]
    rev x1 -> x0, local copies, waits for them, and re-layouts: 1.47 us -> none  [per_device(): values = spread_values(misfit[::-1], receivers[0], width)]
    select_n x2 -> x0, other arithmetic: 1.38 us -> none  [spread_values(): lane = cells % width]
    unnamed x5 -> x8, local copies, waits for them, and re-layouts: 4.79 us -> 4.5 us
where the time goes in v3:
time: 108 us
  Pallas kernels  103 us (95%)
  local copies, waits for them, and re-layouts  4.5 us (4%)
    pallas_call x1, Pallas kernels, per_device(): pl.pallas_call(functools.partial(step_kernel, geometry, subs, shots, stri...  103 us
    unnamed x8, local copies, waits for them, and re-layouts  4.5 us

profile of v3, /device:TPU:0, one launch (start us, length us, event | category | flops | bytes accessed | tf_op | source)
XLA Modules:
  0.0 108.3 jit_solution(11889096176485883056)
XLA Ops:
  0.6 0.0 copy-start.1
  0.6 1.3 %copy.12 = f32[1,12,256]{2,1,0:T(8,128)} copy(f32[1,12,256]{2,0,1:T(1,128)} %param.7) | data formatting | bytes 24576
  2.0 0.0 copy-done.1
  2.0 0.6 copy.11
  2.6 103.1 %shard_map.68 = (f32[4,256,128]{2,1,0:T(8,128)}, f32[4,64,128]{2,1,0:T(8,128)}) custom-call(f32[4,256,128]{2,1,0:T(8,128)} %refs_0_.1, s32[1,256]{1,0:T(1,128)} %refs_1_.1, f32[12,256]{1,0:T(8,128)} %bitcast.7, s32[1,512]{1,0:T(1,128)} %refs_3_.1, f32[12,512]{1,0:T(8,128)} %bitcast.6), custom_call_target="tpu_custom_call" | custom-call | tf_op jit(solution)/shard_map/pallas_call | solution.py:676
  105.7 0.0 copy-start
  105.7 1.9 %copy.15 = f32[4,256,128]{2,1,0:T(8,128)} copy(f32[4,256,128]{2,1,0:T(8,128)} %get-tuple-element.4) | data formatting | bytes 1048576
  107.6 0.0 copy-done
  107.6 0.7 copy.16
Async XLA Ops:
  0.6 1.3 %copy-start.1 = (f32[1,12,512]{2,0,1:T(1,128)S(1)}, f32[1,12,512]{2,0,1:T(1,128)}, u32[]{:S(2)}) copy-start(f32[1,12,512]{2,0,1:T(1,128)} %param.9) | copy-start | bytes 73732
  105.7 1.9 %copy-start = (f32[4,64,128]{2,1,0:T(8,128)S(1)}, f32[4,64,128]{2,1,0:T(8,128)}, u32[]{:S(2)}) copy-start(f32[4,64,128]{2,1,0:T(8,128)} %get-tuple-element.5) | copy-start | bytes 393220

commit v4 on v3

--- a/solution.py
+++ b/solution.py
@@ -126,7 +126,7 @@
         if accumulate is not None:
             accumulate(layer, following[margin : margin + own])
 
-    block = 4
+    block = 8
 
     def block_step(number, carry):
         for part in range(block):

time: 108 us -> 106 us (0.981)
  Pallas kernels: 103 us -> 100 us
    pallas_call x1, Pallas kernels: 103 us -> 100 us  [per_device(): pl.pallas_call(functools.partial(step_kernel, geometry, subs, shots, stri...]
where the time goes in v4:
time: 106 us; the launch traced here: 105 us
  Pallas kernels  100 us (94%)
  local copies, waits for them, and re-layouts  4.5 us (4%)
    pallas_call x1, Pallas kernels, per_device(): pl.pallas_call(functools.partial(step_kernel, geometry, subs, shots, stri...  100 us
    unnamed x8, local copies, waits for them, and re-layouts  4.5 us

profile of v4, /device:TPU:0, one launch (start us, length us, event | category | flops | bytes accessed | tf_op | source)
XLA Modules:
  0.0 105.5 jit_solution(9540238203215068991)
XLA Ops:
  0.6 0.0 copy-start.1
  0.6 1.3 %copy.12 = f32[1,12,256]{2,1,0:T(8,128)} copy(f32[1,12,256]{2,0,1:T(1,128)} %param.7) | data formatting | bytes 24576
  2.0 0.0 copy-done.1
  2.0 0.6 copy.11
  2.6 100.3 %shard_map.68 = (f32[4,256,128]{2,1,0:T(8,128)}, f32[4,64,128]{2,1,0:T(8,128)}) custom-call(f32[4,256,128]{2,1,0:T(8,128)} %refs_0_.1, s32[1,256]{1,0:T(1,128)} %refs_1_.1, f32[12,256]{1,0:T(8,128)} %bitcast.7, s32[1,512]{1,0:T(1,128)} %refs_3_.1, f32[12,512]{1,0:T(8,128)} %bitcast.6), custom_call_target="tpu_custom_call" | custom-call | tf_op jit(solution)/shard_map/pallas_call | solution.py:676
  102.9 0.0 copy-start
  102.9 1.9 %copy.15 = f32[4,256,128]{2,1,0:T(8,128)} copy(f32[4,256,128]{2,1,0:T(8,128)} %get-tuple-element.4) | data formatting | bytes 1048576
  104.8 0.0 copy-done
  104.8 0.7 copy.16
Async XLA Ops:
  0.6 1.3 %copy-start.1 = (f32[1,12,512]{2,0,1:T(1,128)S(1)}, f32[1,12,512]{2,0,1:T(1,128)}, u32[]{:S(2)}) copy-start(f32[1,12,512]{2,0,1:T(1,128)} %param.9) | copy-start | bytes 73732
  102.9 1.9 %copy-start = (f32[4,64,128]{2,1,0:T(8,128)S(1)}, f32[4,64,128]{2,1,0:T(8,128)}, u32[]{:S(2)}) copy-start(f32[4,64,128]{2,1,0:T(8,128)} %get-tuple-element.5) | copy-start | bytes 393220
